TPU v7x, 512 devices: a whole 4x4x16 slice. The times are simulated.
512 devices in a mesh: blk: 128 (over y, x, z_lo), col: 4 (over z_hi, core).
Axes of the slice: x: 4, y: 4, z: 16 (z_hi: 2, z_lo: 8; z = z_hi * 8 + z_lo), core: 2. Of those that a mesh axis runs over, the one named last changes fastest.
Arguments:
- tile_u: bfloat16 [128, 16, 1024, 128], P('blk', 'col'), may hold values from -6 to 6
- tile_v: bfloat16 [128, 16, 1024, 128], P('blk', 'col'), may hold values from -6 to 6
- tile_rank: int32 [128, 16], P('blk', 'col'), may hold values from 32 to 128
- panel_u: bfloat16 [16, 1024, 128], P('col', 'blk'), may hold values from -6 to 6
- panel_v: bfloat16 [16, 1024, 128], P('col', 'blk'), may hold values from -0.1875 to 0.1875
- band_rank: int32 [16], P('col'), may hold values from 32 to 128
- row_u: bfloat16 [128, 1024, 128], P('blk', 'col'), may hold values from -6 to 6
- row_v: bfloat16 [128, 1024, 128], P('blk', 'col'), may hold values from -0.5 to 0.5
- row_rank: int32 [128], P('blk'), may hold values from 32 to 128
- target_rank: int32 [128, 16], P('blk', 'col'), may hold values from 32 to 128
Outputs:
- new_u: bfloat16 [128, 16, 1024, 128], P('blk', 'col')
- new_v: bfloat16 [128, 16, 1024, 128], P('blk', 'col')
All inputs are finite; a program needn't handle non-finite values.
Results may differ from a plain program's by a relative error of at most 0.001.
Values may be sent and summed in bfloat16 or wider, within the bound.
No kernel may reach another device: no remote copies, remote signals or barrier semaphores. Data moves between devices by JAX's collectives and lax.ppermute only.
A program may use at most 64 MiB of HBM per device.

v0:
```python
import math

import jax
import jax.numpy as jnp
from jax import lax
from jax.sharding import PartitionSpec as P

HIGH = lax.Precision.HIGHEST


def pair_columns(first, second):
    joined = jnp.stack([first, second], axis=-1)
    return joined.reshape(joined.shape[:-2] + (joined.shape[-2] * 2,))


def on_device(
    tile_u, tile_v, tile_rank, panel_u, panel_v, band_rank, row_u, row_v, row_rank, target_rank
):
    width = tile_u.shape[3]
    order = tile_u.shape[2]
    lane = jnp.arange(width)
    row_u_all, row_v_all = (
        lax.all_gather(row_u, "col", axis=1, tiled=True),
        lax.all_gather(row_v, "col", axis=1, tiled=True),
    )
    row_keep = (lane < row_rank[0]).astype(jnp.bfloat16)
    tile_keep = (lane[None, :] < tile_rank[0][:, None]).astype(jnp.bfloat16)
    band_keep = (lane[None, :] < band_rank[:, None]).astype(jnp.bfloat16)
    left_row = row_u_all[0] * row_keep[None, :]
    right_row = row_v_all[0] * row_keep[None, :]
    left_tile = tile_u[0] * tile_keep[:, None, :]
    right_tile = (tile_v[0] * tile_keep[:, None, :]).astype(jnp.float32)
    left = pair_columns(left_tile, jnp.broadcast_to(left_row, left_tile.shape))
    spare = 1.0 - pair_columns(
        tile_keep.astype(jnp.float32),
        jnp.broadcast_to(row_keep.astype(jnp.float32), tile_keep.shape),
    )
    gram = jnp.einsum("jnk,jnl->jkl", left, left, preferred_element_type=jnp.float32)
    gram = gram + spare[:, :, None] * jnp.eye(2 * width, dtype=jnp.float32)[None]
    lower = jnp.linalg.cholesky(gram)
    ortho = lax.linalg.triangular_solve(
        lower, left.astype(jnp.float32), left_side=False, lower=True, transpose_a=True
    )
    target_keep = (lane[None, :] < target_rank[0][:, None]).astype(jnp.float32)
    scale = math.sqrt(order)
    new_u = ortho[:, :, :width] * scale * target_keep[:, None, :]
    head = jnp.transpose(lower, (0, 2, 1))[:, :width, :]
    masked = lax.all_gather(panel_v, "blk", axis=1, tiled=True) * band_keep[:, None, :]
    core = jnp.einsum("nk,jnl->jkl", right_row, masked, preferred_element_type=jnp.float32)
    masked = (lax.all_gather(panel_u, "blk", axis=1, tiled=True) * band_keep[:, None, :]).astype(
        jnp.float32
    )
    panel_part = -jnp.einsum("jnl,jkl->jnk", masked, core, precision=HIGH)
    right = pair_columns(right_tile, panel_part)
    new_v = jnp.einsum("jnc,jmc->jnm", right, head, precision=HIGH)
    new_v = new_v / scale * target_keep[:, None, :]
    return (new_u[None].astype(jnp.bfloat16), new_v[None].astype(jnp.bfloat16))


def solution(mesh):
    return jax.shard_map(
        on_device,
        mesh=mesh,
        in_specs=(
            P("blk", "col", None, None),
            P("blk", "col", None, None),
            P("blk", "col"),
            P("col", "blk", None),
            P("col", "blk", None),
            P("col"),
            P("blk", "col", None),
            P("blk", "col", None),
            P("blk"),
            P("blk", "col"),
        ),
        out_specs=(P("blk", "col", None, None), P("blk", "col", None, None)),
        check_vma=False,
    )
```

profile of v0, /device:TPU:0, one launch (start us, length us, event | category | flops | bytes accessed | tf_op | source)
XLA Modules:
  0.0 1489.5 jit_solution(16224905090868554717)
XLA Ops:
  7.2 0.0 copy-start.4
  7.2 0.0 all-gather.5.cloned.1.call-start
  7.2 0.7 all-gather.5.cloned.1.call-update
  7.9 0.0 all-gather.3.cloned.1.call-start
  8.0 0.7 all-gather.3.cloned.1.call-update
  8.7 0.7 fusion.24
  9.4 0.7 fusion.29
  10.1 0.7 fusion.32
  10.8 0.6 iota_compare_fusion.3
  11.5 0.6 iota_compare_fusion.2
  12.1 14.8 all_gather.12
  27.6 0.0 copy-start.8
  27.6 0.1 copy.61
  27.8 0.0 copy-done.4
  27.8 0.5 copy.74
  28.3 1.5 copy.60
  29.8 0.0 copy-done.8
  29.8 1.6 fusion.9
  31.4 0.1 stack_broadcast_in_dim.6
  31.6 0.2 pad_maximum_fusion.1
  31.8 2.9 copy.62
  34.7 3.0 copy.63
  37.7 0.9 fusion.35
  38.6 1.3 copy.68
  39.9 0.6 maximum_subtract_fusion
  40.5 0.8 copy.66
  41.3 0.7 copy.67
  42.0 1.6 fusion.11
  43.6 0.0 copy-start.2
  43.6 1.0 copy-done.2
  44.6 46.9 %custom-call.16 = f32[4,128,128]{2,1,0:T(8,128)S(1)} custom-call(f32[4,128,128]{2,1,0:T(8,128)S(1)} %cholesky.122), custom_call_target="Cholesky" | custom-call | tf_op jit(solution)/shard_map/jit(cholesky)/cholesky | solution.py:40
  91.5 0.0 copy-start.5
  91.5 0.1 cholesky.117
  91.6 0.7 select_bitcast_fusion
  92.3 40.8 %custom-call.17 = f32[4,1,128,128]{2,3,1,0:T(8,128)} custom-call(f32[4,1,128,128]{3,2,1,0:T(8,128)} %select_bitcast_fusion), custom_call_target="InvertDiagBlocksLowerTriangular" | custom-call | tf_op jit(solution)/shard_map/jit(cholesky)/cholesky | solution.py:40
  133.1 1.4 constant_dynamic-update-slice_fusion.1
  134.5 2.3 convolution_subtract_fusion
  136.8 48.4 %custom-call.18 = f32[4,128,128]{2,1,0:T(8,128)} custom-call(f32[4,128,128]{2,1,0:T(8,128)} %convolution_subtract_fusion), custom_call_target="Cholesky" | custom-call | tf_op jit(solution)/shard_map/jit(cholesky)/cholesky | solution.py:40
  185.2 1.0 select_reduce_fusion
  186.2 0.0 copy-start.1
  186.2 0.1 compare_reduce_fusion.1
  186.3 0.1 compare_reduce_fusion
  186.4 0.7 copy-done.1
  187.2 0.0 copy-done.5
  187.2 2.4 fusion.15
  189.6 0.1 triangular_solve.53
  189.7 5.2 while.1
  189.7 0.6 fusion.42
  190.3 2.0 bitcast_dynamic-update-slice_fusion.2
  192.3 0.6 fusion.42
  192.9 2.0 bitcast_dynamic-update-slice_fusion.2
  194.9 79.4 %custom-call.19 = f32[4,2,128,128]{2,3,1,0:T(8,128)S(1)} custom-call(f32[4,2,128,128]{3,2,1,0:T(8,128)} %bitcast.74), custom_call_target="InvertDiagBlocksLowerTriangular" | custom-call | tf_op jit(solution)/shard_map/triangular_solve | solution.py:41
  274.4 14.9 all_gather.15
  289.2 0.1 fusion.27
  289.3 2.0 fusion.7
  291.3 0.1 fusion.31
  291.4 451.7 %all-gather.5.cloned.1.call-done = bf16[4,1024,128]{2,1,0:T(8,128)(2,1)} async-done(((bf16[4,8,128]{2,1,0:T(8,128)(2,1)}), bf16[4,1024,128]{2,1,0:T(8,128)(2,1)}) %all-gather.5.cloned.1.call-update) | async-done | bytes 1048592 | tf_op jit(solution)/shard_map/all_gather | solution.py:48
  743.1 1.6 fusion.12
  744.6 723.3 %all-gather.3.cloned.1.call-done = bf16[4,1024,128]{2,1,0:T(8,128)(2,1)} async-done(((bf16[4,8,128]{2,1,0:T(8,128)(2,1)}), bf16[4,1024,128]{2,1,0:T(8,128)(2,1)}) %all-gather.3.cloned.1.call-update) | async-done | bytes 1048592 | tf_op jit(solution)/shard_map/all_gather | solution.py:50
  1467.9 2.2 negate_bitcast_fusion
  1470.2 0.3 pad_maximum_fusion
  1470.5 0.0 copy-start.3
  1470.5 2.7 copy.77
  1473.2 9.4 fusion.4
  (24 shorter events, 0.1 us)
Async XLA Ops:
  7.2 20.6 %copy-start.4 = (bf16[1,4,1024,128]{3,2,1,0:T(8,128)(2,1)S(1)}, bf16[1,4,1024,128]{3,2,1,0:T(8,128)(2,1)}, u32[]{:S(2)}) copy-start(bf16[1,4,1024,128]{3,2,1,0:T(8,128)(2,1)} %param.11) | copy-start | bytes 3145732
  7.2 735.9 %all-gather.5.cloned.1.call-start = ((), (), s32[]{:S(2)}) async-start(), calls=%async_computation.1 | async-start | bytes 1056768 | tf_op jit(solution)/shard_map/all_gather | solution.py:48
  7.9 1460.0 %all-gather.3.cloned.1.call-start = ((), (), s32[]{:S(2)}) async-start(), calls=%async_computation | async-start | bytes 1056768 | tf_op jit(solution)/shard_map/all_gather | solution.py:50
  27.6 2.2 copy-start.8
  42.0 49.6 %copy-start.7 = (pred[128,128]{1,0:T(8,128)(4,1)S(1)}, pred[128,128]{1,0:T(8,128)(4,1)}, u32[]{:S(2)}) copy-start(pred[128,128]{1,0:T(8,128)(4,1)} %iota_compare_fusion.3) | copy-start | bytes 49156
  43.6 1.0 copy-start.2
  91.5 95.7 %copy-start.5 = (pred[256,256]{1,0:T(8,128)(4,1)S(1)}, pred[256,256]{1,0:T(8,128)(4,1)}, u32[]{:S(2)}) copy-start(pred[256,256]{1,0:T(8,128)(4,1)} %iota_compare_fusion.2) | copy-start | bytes 196612
  186.2 1.0 copy-start.1
  189.6 84.8 %copy-start.6 = (bf16[1,256,128]{2,1,0:T(8,128)(2,1)S(1)}, bf16[1,256,128]{2,1,0:T(8,128)(2,1)}, u32[]{:S(2)}) copy-start(bf16[1,256,128]{2,1,0:T(8,128)(2,1)} %param.17) | copy-start | bytes 196612
  189.6 99.6 %copy-start.10 = (s32[1,4]{1,0:T(1,128)S(1)}, s32[1,4]{1,0:T(1,128)}, u32[]{:S(2)}) copy-start(s32[1,4]{1,0:T(1,128)} %param.19) | copy-start | bytes 52
  189.7 101.6 %copy-start.11 = (s32[4]{0:T(128)S(1)}, s32[4]{0:T(128)}, u32[]{:S(2)}) copy-start(s32[4]{0:T(128)} %param.15) | copy-start | bytes 52
  189.7 553.4 %copy-start.9 = (bf16[128]{0:T(256)(128)(2,1)S(1)}, bf16[128]{0:T(256)(128)(2,1)}, u32[]{:S(2)}) copy-start(bf16[128]{0:T(256)(128)(2,1)} %copy-done.8) | copy-start | bytes 772
  744.6 725.5 %copy-start = (f32[4,1024,128,1]{1,2,0,3:T(8,128)S(1)}, f32[4,1024,128,1]{1,2,0,3:T(8,128)}, u32[]{:S(2)}) copy-start(f32[4,1024,128,1]{1,2,0,3:T(8,128)} %get-tuple-element.25) | copy-start | bytes 6291460
  1470.5 2.7 copy-start.3
Sparse Core Ops, SparseCore 0:
  10.0 732.9 all-gather.4
  745.1 722.8 all-gather.2
where the time goes:
time: 1490 us
  waiting for transfers between devices  1180 us (79%)
  other arithmetic  228 us (15%)
  blocking collectives  29.7 us (2%)
  local copies, waits for them, and re-layouts  20.8 us (1%)
  matrix products  19.8 us (1%)
  between operations  15 us (1%)
    all_gather x1, waiting for transfers between devices, on_device(): lax.all_gather(panel_u, 'blk', axis=1, tiled=True) * band_keep[:, None, :]  723 us
    all_gather x1, waiting for transfers between devices, on_device(): lax.all_gather(panel_v, 'blk', axis=1, tiled=True) * band_keep[:, None, :]  452 us
    another operation x10, other arithmetic, on_device(): lower = jnp.linalg.cholesky(gram)  139 us
    another operation x3, other arithmetic, on_device(): lax.linalg.triangular_solve(lower, left.astype(jnp.float32), left_side=Fa...  80.1 us
  transfers between devices with their start and end apart: 2, of which 2 were waited for; matrix products, arithmetic and copies ran while one was open for 17% of the time, Pallas kernels for 0%

commit v1 on v0

v1 whole, which is shorter than its diff:
```python
import math

import jax
import jax.numpy as jnp
from jax import lax
from jax.experimental import pallas as pl
from jax.experimental.pallas import tpu as pltpu
from jax.sharding import Mesh, PartitionSpec as P

F32, BF16 = jnp.float32, jnp.bfloat16
HIGH = lax.Precision.HIGHEST
STEP = 8


def dot(a, b, dims, precision=None):
    return lax.dot_general(
        a, b, (dims, ((), ())), precision=precision, preferred_element_type=F32
    )


def three_parts(x):
    high = x.astype(BF16).astype(F32)
    rest = x - high
    middle = rest.astype(BF16).astype(F32)
    return high, middle, rest - middle


def spread(row):
    return jnp.broadcast_to(row, (STEP, row.shape[1]))


def factor_panel(panel, inverse, first):
    width = panel.shape[1]
    sub = lax.broadcasted_iota(jnp.int32, (STEP, width), 0)
    column = [
        jnp.broadcast_to(panel[:, first + s : first + s + 1], (STEP, width)) for s in range(STEP)
    ]
    for s in range(STEP - 1):
        ratio = jnp.where(sub > s, column[s] / spread(column[s][s : s + 1]), 0.0)
        panel = panel - ratio * spread(panel[s : s + 1])
        inverse = inverse - ratio * spread(inverse[s : s + 1])
        for u in range(s + 1, STEP):
            column[u] = column[u] - ratio * spread(column[u][s : s + 1])
    pivot = column[0]
    for s in range(1, STEP):
        pivot = jnp.where(sub == s, column[s], pivot)
    scale = lax.rsqrt(pivot)
    scale = scale * (1.5 - 0.5 * pivot * scale * scale)
    return panel * scale, inverse * scale


def left_kernel(
    tile_rank, row_rank, target_rank, place, tile_u, near, far, new_u, head, gram, lower_inv
):
    tiles, order, width = tile_u.shape
    quarter = order // 4
    lane = lax.broadcasted_iota(jnp.int32, (width, width), 1)
    sub = lax.broadcasted_iota(jnp.int32, (width, width), 0)
    rows = []
    for q in range(4):
        mine, other = place[0] ^ (q // 2), place[1] ^ (q % 2)
        rows.append(jnp.where(other == 0, near[mine, 0], far[mine, 0]))
    left_row = jnp.concatenate(rows, axis=0)
    pick_row = jnp.where((lane == 2 * sub + 1) & (sub < row_rank[0]), 1.0, 0.0)
    firsts, sides = [], []
    for t in range(tiles):
        pick_tile = jnp.where((lane == 2 * sub) & (sub < tile_rank[0, t]), 1.0, 0.0)
        pick = jnp.concatenate([pick_tile, pick_row], axis=0).astype(BF16)
        both = jnp.concatenate([tile_u[t], left_row], axis=1)
        first = dot(both, pick, ((1,), (0,))).astype(BF16)
        side = dot(first, jnp.concatenate([both, first], axis=1), ((0,), (0,)))
        half = sub // 2
        rank = jnp.where(sub % 2 == 0, tile_rank[0, t], row_rank[0])
        unit = jnp.where(lane == sub, 1.0, 0.0)
        gram[t, :, :width] = side[:, 2 * width :] + jnp.where(half >= rank, unit, 0.0)
        gram[t, :, width:] = unit
        firsts.append(first)
        tile_side = jnp.where(lane < tile_rank[0, t], side[:, :width], 0.0)
        row_side = jnp.where(lane < row_rank[0], side[:, width : 2 * width], 0.0)
        sides.append(jnp.concatenate([tile_side, row_side], axis=1))
    for first in range(0, width, STEP):
        later = first + STEP
        for t in range(tiles):
            upper, inverse = factor_panel(
                gram[t, first:later, :width], gram[t, first:later, width:], first
            )
            lower_inv[t, first:later, :] = inverse
            if later < width:
                uh, um, ul = three_parts(upper)
                ih, im, il = three_parts(inverse)
                a = jnp.concatenate([uh, uh, um, uh, um, ul], axis=0).astype(BF16)
                b = jnp.concatenate(
                    [
                        jnp.concatenate([uh, um, uh, ul, um, uh], axis=0),
                        jnp.concatenate([ih, im, ih, il, im, ih], axis=0),
                    ],
                    axis=1,
                ).astype(BF16)
                change = dot(a, b, ((0,), (0,)))
                gram[t, later:, :] = gram[t, later:, :] - change[later:, :]
    scale = math.sqrt(order)
    for t in range(tiles):
        solved = jnp.where(sub < target_rank[0, t], lower_inv[t], 0.0)
        head[t] = dot(solved, sides[t], ((1,), (0,)), HIGH) / scale
        solved = solved * scale
        high = solved.astype(BF16)
        low = (solved - high.astype(F32)).astype(BF16)
        new_u[0, t] = dot(
            jnp.concatenate([firsts[t], firsts[t]], axis=1),
            jnp.concatenate([high, low], axis=1),
            ((1,), (1,)),
        ).astype(BF16)


def right_kernel(band_rank, place, tile_v, near, far, panels, head, new_v):
    tiles, order, width = tile_v.shape
    rows = []
    for q in range(4):
        mine, other = place[0] ^ (q // 2), place[1] ^ (q % 2)
        rows.append(jnp.where(other == 0, near[mine, 1], far[mine, 1]))
    right_row = jnp.concatenate(rows, axis=0)
    lane = lax.broadcasted_iota(jnp.int32, (width, width), 1)

    def panel(which):
        found = []
        for pair in range(0, tiles, 2):
            at = (which * tiles + pair) * STEP
            wide = panels[:, at : at + 2 * STEP, :].astype(F32)
            found.append(wide[:, :STEP].reshape(order, width).astype(BF16))
            found.append(wide[:, STEP:].reshape(order, width).astype(BF16))
        return found

    panel_u, panel_v = panel(0), panel(1)
    core = dot(right_row, jnp.concatenate(panel_v, axis=1), ((0,), (0,)))
    for t in range(tiles):
        mixed = dot(head[t, :, width:], core[:, t * width : (t + 1) * width], ((1,), (0,)), HIGH)
        mixed = jnp.where(lane < band_rank[t], -mixed, 0.0)
        weight = jnp.concatenate([head[t, :, :width], mixed], axis=1)
        high = weight.astype(BF16)
        low = (weight - high.astype(F32)).astype(BF16)
        both = jnp.concatenate([tile_v[t], panel_u[t]], axis=1)
        value = dot(both, jnp.concatenate([high, low], axis=0), ((1,), (1,)))
        new_v[0, t] = (value[:, :width] + value[:, width:]).astype(BF16)


SMEM = pl.BlockSpec(memory_space=pltpu.SMEM)
VMEM = pl.BlockSpec(memory_space=pltpu.VMEM)
LIMIT = 40 * 1024 * 1024


def left_side(tile_rank, row_rank, target_rank, place, tile_u, near, far):
    tiles, order, width = tile_u.shape
    return pl.pallas_call(
        left_kernel,
        out_shape=(
            jax.ShapeDtypeStruct((1, tiles, order, width), BF16),
            jax.ShapeDtypeStruct((tiles, width, 2 * width), F32),
        ),
        in_specs=[SMEM] * 4 + [VMEM] * 3,
        out_specs=(VMEM, VMEM),
        scratch_shapes=[
            pltpu.VMEM((tiles, width, 2 * width), F32),
            pltpu.VMEM((tiles, width, width), F32),
        ],
        compiler_params=pltpu.CompilerParams(vmem_limit_bytes=LIMIT),
        cost_estimate=pl.CostEstimate(
            flops=int(1e10), bytes_accessed=int(40e6), transcendentals=0
        ),
        name="left_side",
    )(tile_rank, row_rank, target_rank, place, tile_u, near, far)


def right_side(band_rank, place, tile_v, near, far, panels, head):
    tiles, order, width = tile_v.shape
    return pl.pallas_call(
        right_kernel,
        out_shape=jax.ShapeDtypeStruct((1, tiles, order, width), BF16),
        in_specs=[SMEM] * 2 + [VMEM] * 5,
        out_specs=VMEM,
        compiler_params=pltpu.CompilerParams(vmem_limit_bytes=LIMIT),
        cost_estimate=pl.CostEstimate(
            flops=int(2e9), bytes_accessed=int(10e6), transcendentals=0
        ),
        name="right_side",
    )(band_rank, place, tile_v, near, far, panels, head)


def from_all(x, axes, size):
    copies = jnp.broadcast_to(x[None], (size,) + x.shape)
    return lax.all_to_all(copies, axes, 0, 0, tiled=True)


def swap(x, axis):
    return lax.ppermute(x, axis, [(0, 1), (1, 0)])


def on_device(
    tile_u, tile_v, tile_rank, panel_u, panel_v, band_rank, row_u, row_v, row_rank, target_rank
):
    tiles, share, width = panel_u.shape
    row = jnp.concatenate([row_u, row_v], axis=0)
    panel = jnp.concatenate([panel_u, panel_v], axis=0).reshape(2 * tiles * share, width)
    across = swap(row, "zh")
    line = from_all(panel, "z", 8)
    panels = from_all(line, ("y", "x"), 16)
    near = jnp.stack([row, across])
    far = swap(near, "core")
    place = jnp.stack([lax.axis_index("zh"), lax.axis_index("core")]).astype(jnp.int32)
    new_u, head = left_side(tile_rank, row_rank, target_rank, place, tile_u[0], near, far)
    panels = panels.reshape(128, 2 * tiles * share, width)
    new_v = right_side(band_rank, place, tile_v[0], near, far, panels, head)
    return new_u, new_v


def solution(mesh):
    fine = Mesh(mesh.devices.reshape(4, 4, 8, 2, 2), ("y", "x", "z", "zh", "core"))
    blk, col = ("y", "x", "z"), ("zh", "core")
    return jax.shard_map(
        on_device,
        mesh=fine,
        in_specs=(
            P(blk, col, None, None),
            P(blk, col, None, None),
            P(blk, col),
            P(col, blk, None),
            P(col, blk, None),
            P(col),
            P(blk, col, None),
            P(blk, col, None),
            P(blk),
            P(blk, col),
        ),
        out_specs=(P(blk, col, None, None), P(blk, col, None, None)),
        check_vma=False,
    )
```

time: 1490 us -> 79.6 us (0.05)
  the two profiles are of different devices: /device:TPU:0 before, /device:TPU:1 now
where the time goes in v1:
time: 79.6 us; the launch traced here: 79.2 us
  blocking collectives  23.2 us (29%)
  starting transfers between devices  22.2 us (28%)
  Pallas kernels  14.7 us (18%)
  waiting for transfers between devices  12 us (15%)
  local copies, waits for them, and re-layouts  4.97 us (6%)
  between operations  1.37 us (2%)
  other arithmetic  0.82 us (1%)
    all_to_all x1, blocking collectives, from_all(): return lax.all_to_all(copies, axes, 0, 0, tiled=True)  23.2 us
    ppermute x2, starting transfers between devices, swap(): return lax.ppermute(x, axis, [(0, 1), (1, 0)])  15.3 us
    ppermute x2, waiting for transfers between devices, swap(): return lax.ppermute(x, axis, [(0, 1), (1, 0)])  12 us
    pallas_call x1, Pallas kernels, left_side(): pl.pallas_call(left_kernel, out_shape=(jax.ShapeDtypeStruct((1, tiles, or...  11.1 us
    all_to_all x1, starting transfers between devices, from_all(): return lax.all_to_all(copies, axes, 0, 0, tiled=True)  6.9 us
    pallas_call x1, Pallas kernels, right_side(): pl.pallas_call(right_kernel, out_shape=jax.ShapeDtypeStruct((1, tiles, or...  3.6 us
    unnamed x19, local copies, waits for them, and re-layouts  3.09 us
    broadcast_in_dim x2, local copies, waits for them, and re-layouts, from_all(): copies = jnp.broadcast_to(x[None], (size,) + x.shape)  1.87 us
  transfers between devices with their start and end apart: 3, of which 2 were waited for; matrix products, arithmetic and copies ran while one was open for 0% of the time, Pallas kernels for 14%

profile of v1, /device:TPU:1, one launch (start us, length us, event | category | flops | bytes accessed | tf_op | source)
XLA Modules:
  0.0 79.2 jit_solution(10700876445909920009)
XLA Ops:
  0.6 0.7 maximum_bitcast_fusion
  1.4 23.2 %all_to_all.10 = bf16[8,64,128]{2,1,0:T(8,128)(2,1)S(1)} all-to-all(bf16[8,64,128]{2,1,0:T(8,128)(2,1)S(1)} %broadcast_in_dim.14), channel_id=1, replica_groups=mesh['y'=4,'x'=4,'z'=8,'zh'=2,'core'=2] {'z'}, dimensions={0} | all-to-all | bytes 262144 | tf_op jit(solution)/shard_map/all_to_all | solution.py:190
  24.6 1.9 %broadcast_in_dim.15 = bf16[16,8,64,128]{3,2,1,0:T(8,128)(2,1)} broadcast(bf16[8,64,128]{2,1,0:T(8,128)(2,1)S(1)} %all_to_all.10), dimensions={1,2,3} | broadcast | bytes 2228224 | tf_op jit(solution)/shard_map/broadcast_in_dim | solution.py:189
  26.4 0.0 copy-start.7
  26.4 0.0 copy-start.8
  26.4 0.0 copy-start
  26.4 0.0 copy-start.2
  26.4 0.0 copy-start.3
  26.5 6.9 %all-to-all-start.1 = ((bf16[16,8,64,128]{3,2,1,0:T(8,128)(2,1)}), bf16[16,8,64,128]{3,2,1,0:T(8,128)(2,1)S(1)}, u32[]{:S(2)}, u32[]{:S(2)}) async-start(bf16[16,8,64,128]{3,2,1,0:T(8,128)(2,1)} %broadcast_in_dim.15), calls=%async_computation.1 | async-start | bytes 4194304 | tf_op jit(solution)/shard_map/all_to_all | solution.py:190
  33.4 0.0 copy-done.7
  33.4 0.0 copy-done.8
  33.4 7.9 %collective-permute-start = (bf16[2,256,128]{2,1,0:T(8,128)(2,1)S(1)}, bf16[2,256,128]{2,1,0:T(8,128)(2,1)S(1)}, u32[]{:S(2)}, u32[]{:S(2)}) collective-permute-start(bf16[2,256,128]{2,1,0:T(8,128)(2,1)S(1)} %constant_dynamic-update-slice_fusion), channel_id=1, source_target_pairs={{0,2},{2,0},{1,3},{3,1},{4,6},{6,4},{5,7},{7,5},{8,10},{10,8},{9,1... | collective-permute-start | bytes 393224 | tf_op jit(solution)/shard_map/ppermute | solution.py:194
  41.4 11.5 %collective-permute-done = bf16[2,256,128]{2,1,0:T(8,128)(2,1)S(1)} collective-permute-done((bf16[2,256,128]{2,1,0:T(8,128)(2,1)S(1)}, bf16[2,256,128]{2,1,0:T(8,128)(2,1)S(1)}, u32[]{:S(2)}, u32[]{:S(2)}) %collective-permute-start) | collective-permute-done | bytes 131104 | tf_op jit(solution)/shard_map/ppermute | solution.py:194
  52.8 7.3 %collective-permute-start.1 = (bf16[2,2,256,128]{3,2,1,0:T(8,128)(2,1)S(1)}, bf16[2,2,256,128]{3,2,1,0:T(8,128)(2,1)}, u32[]{:S(2)}, u32[]{:S(2)}) collective-permute-start(bf16[2,2,256,128]{3,2,1,0:T(8,128)(2,1)S(1)} %pad_maximum_fusion.near), channel_id=1, source_target_pairs={{0,1},{1,0},{2,3},{3,2},{4,5},{5,4},{6,7},{7,6},{8,9},{9,8},{10,11... | collective-permute-start | bytes 786440 | tf_op jit(solution)/shard_map/ppermute | solution.py:194
  60.8 0.1 pad_add_fusion.place
  60.9 0.5 collective-permute-done.1.far
  61.4 0.0 copy-done
  61.4 0.0 copy-done.2
  61.4 0.0 copy-done.3
  61.5 0.0 copy-start.4
  61.5 11.1 %left_side.1 = (bf16[1,4,1024,128]{3,2,1,0:T(8,128)(2,1)}, f32[4,128,256]{2,1,0:T(8,128)S(1)}) custom-call(s32[1,4]{1,0:T(1,128)S(1)} %copy-done.2, s32[1]{0:T(128)S(6)} %copy.13.row_rank, s32[1,4]{1,0:T(1,128)S(1)} %copy-done.3, s32[2]{0:T(128)S(1)} %pad_add_fusion.place, bf16[4,1024,128]{2,1,0:T(8,128)(2,1)S(1)} %bitcast.10, ...), custom_call_target="tpu_custom_call" | custom-call | flops 10000000000 | bytes 40000000 | tf_op jit(solution)/shard_map/left_side/pallas_call | solution.py:153
  72.5 0.0 copy-start.5
  72.5 0.8 copy-done.5
  73.3 0.0 all-to-all-done.1
  73.3 0.0 copy-done.4
  73.3 0.0 copy-start.1
  73.3 1.2 %copy-done.1 = bf16[1,4,1024,128]{3,2,1,0:T(8,128)(2,1)S(1)} copy-done((bf16[1,4,1024,128]{3,2,1,0:T(8,128)(2,1)S(1)}, bf16[1,4,1024,128]{3,2,1,0:T(8,128)(2,1)}, u32[]{:S(2)}) %copy-start.1) | copy-done | bytes 1048600
  74.6 0.0 copy-start.6
  74.6 1.0 %copy-done.6 = f32[4,128,256]{2,1,0:T(8,128)S(1)} copy-done((f32[4,128,256]{2,1,0:T(8,128)S(1)}, f32[4,128,256]{2,1,0:T(8,128)}, u32[]{:S(2)}) %copy-start.6) | copy-done | bytes 524312
  75.6 3.6 %right_side.1 = bf16[1,4,1024,128]{3,2,1,0:T(8,128)(2,1)} custom-call(s32[4]{0:T(128)S(1)} %copy-done.4, s32[2]{0:T(128)S(1)} %pad_add_fusion.place, bf16[4,1024,128]{2,1,0:T(8,128)(2,1)S(1)} %bitcast.11, bf16[2,2,256,128]{3,2,1,0:T(8,128)(2,1)S(1)} %pad_maximum_fusion.near, bf16[2,2,256,128]{3,2,1,0:T(8,128)(2,1)} %collective-permute-done.1.far, ...), custom_call_target="tpu_custom_call" | custom-call | flops 2000000000 | bytes 10000000 | tf_op jit(solution)/shard_map/right_side/pallas_call | solution.py:175
  (4 shorter events, 0.1 us)
Async XLA Ops:
  26.4 6.9 %copy-start.7 = (bf16[1,256,128]{2,1,0:T(8,128)(2,1)S(1)}, bf16[1,256,128]{2,1,0:T(8,128)(2,1)}, u32[]{:S(2)}) copy-start(bf16[1,256,128]{2,1,0:T(8,128)(2,1)} %param.16) | copy-start | bytes 196612
  26.4 7.0 %copy-start.8 = (bf16[1,256,128]{2,1,0:T(8,128)(2,1)S(1)}, bf16[1,256,128]{2,1,0:T(8,128)(2,1)}, u32[]{:S(2)}) copy-start(bf16[1,256,128]{2,1,0:T(8,128)(2,1)} %param.17) | copy-start | bytes 196612
  26.4 35.0 %copy-start = (bf16[1,4,1024,128]{3,2,1,0:T(8,128)(2,1)S(1)}, bf16[1,4,1024,128]{3,2,1,0:T(8,128)(2,1)}, u32[]{:S(2)}) copy-start(bf16[1,4,1024,128]{3,2,1,0:T(8,128)(2,1)} %param.10) | copy-start | bytes 3145732
  26.4 35.0 %copy-start.2 = (s32[1,4]{1,0:T(1,128)S(1)}, s32[1,4]{1,0:T(1,128)}, u32[]{:S(2)}) copy-start(s32[1,4]{1,0:T(1,128)} %tile_rank.1) | copy-start | bytes 52
  26.4 35.0 %copy-start.3 = (s32[1,4]{1,0:T(1,128)S(1)}, s32[1,4]{1,0:T(1,128)}, u32[]{:S(2)}) copy-start(s32[1,4]{1,0:T(1,128)} %target_rank.1) | copy-start | bytes 52
  26.5 46.9 %all-to-all-start.1 = ((bf16[16,8,64,128]{3,2,1,0:T(8,128)(2,1)}), bf16[16,8,64,128]{3,2,1,0:T(8,128)(2,1)S(1)}, u32[]{:S(2)}, u32[]{:S(2)}) async-start(bf16[16,8,64,128]{3,2,1,0:T(8,128)(2,1)} %broadcast_in_dim.15), calls=%async_computation.1 | async-start | bytes 4194304 | tf_op jit(solution)/shard_map/all_to_all | solution.py:190
  33.4 19.4 %collective-permute-start = (bf16[2,256,128]{2,1,0:T(8,128)(2,1)S(1)}, bf16[2,256,128]{2,1,0:T(8,128)(2,1)S(1)}, u32[]{:S(2)}, u32[]{:S(2)}) collective-permute-start(bf16[2,256,128]{2,1,0:T(8,128)(2,1)S(1)} %constant_dynamic-update-slice_fusion), channel_id=1, source_target_pairs={{0,2},{2,0},{1,3},{3,1},{4,6},{6,4},{5,7},{7,5},{8,10},{10,8},{9,1... | collective-permute-start | bytes 393224 | tf_op jit(solution)/shard_map/ppermute | solution.py:194
  52.8 8.6 %collective-permute-start.1 = (bf16[2,2,256,128]{3,2,1,0:T(8,128)(2,1)S(1)}, bf16[2,2,256,128]{3,2,1,0:T(8,128)(2,1)}, u32[]{:S(2)}, u32[]{:S(2)}) collective-permute-start(bf16[2,2,256,128]{3,2,1,0:T(8,128)(2,1)S(1)} %pad_maximum_fusion.near), channel_id=1, source_target_pairs={{0,1},{1,0},{2,3},{3,2},{4,5},{5,4},{6,7},{7,6},{8,9},{9,8},{10,11... | collective-permute-start | bytes 786440 | tf_op jit(solution)/shard_map/ppermute | solution.py:194
  61.5 11.9 %copy-start.4 = (s32[4]{0:T(128)S(1)}, s32[4]{0:T(128)}, u32[]{:S(2)}) copy-start(s32[4]{0:T(128)} %band_rank.1) | copy-start | bytes 52
  72.5 0.8 %copy-start.5 = (f32[4,128,256]{2,1,0:T(8,128)}, f32[4,128,256]{2,1,0:T(8,128)S(1)}, u32[]{:S(2)}) copy-start(f32[4,128,256]{2,1,0:T(8,128)S(1)} %get-tuple-element.5.head) | copy-start | bytes 1572868
  73.3 1.2 %copy-start.1 = (bf16[1,4,1024,128]{3,2,1,0:T(8,128)(2,1)S(1)}, bf16[1,4,1024,128]{3,2,1,0:T(8,128)(2,1)}, u32[]{:S(2)}) copy-start(bf16[1,4,1024,128]{3,2,1,0:T(8,128)(2,1)} %param.11) | copy-start | bytes 3145732
  74.6 1.0 %copy-start.6 = (f32[4,128,256]{2,1,0:T(8,128)S(1)}, f32[4,128,256]{2,1,0:T(8,128)}, u32[]{:S(2)}) copy-start(f32[4,128,256]{2,1,0:T(8,128)} %copy-done.5) | copy-start | bytes 1572868

commit v2 on v1

--- a/solution.py
+++ b/solution.py
@@ -112,7 +112,7 @@
         ).astype(BF16)
 
 
-def right_kernel(band_rank, place, tile_v, near, far, panels, head, new_v):
+def right_kernel(band_rank, place, tile_v, near, far, panels, head, new_v, out_at, sems):
     tiles, order, width = tile_v.shape
     rows = []
     for q in range(4):
@@ -130,8 +130,9 @@
             found.append(wide[:, STEP:].reshape(order, width).astype(BF16))
         return found
 
-    panel_u, panel_v = panel(0), panel(1)
-    core = dot(right_row, jnp.concatenate(panel_v, axis=1), ((0,), (0,)))
+    core = dot(right_row, jnp.concatenate(panel(1), axis=1), ((0,), (0,)))
+    panel_u = panel(0)
+    stores = []
     for t in range(tiles):
         mixed = dot(head[t, :, width:], core[:, t * width : (t + 1) * width], ((1,), (0,)), HIGH)
         mixed = jnp.where(lane < band_rank[t], -mixed, 0.0)
@@ -140,12 +141,17 @@
         low = (weight - high.astype(F32)).astype(BF16)
         both = jnp.concatenate([tile_v[t], panel_u[t]], axis=1)
         value = dot(both, jnp.concatenate([high, low], axis=0), ((1,), (1,)))
-        new_v[0, t] = (value[:, :width] + value[:, width:]).astype(BF16)
+        out_at[t] = (value[:, :width] + value[:, width:]).astype(BF16)
+        stores.append(pltpu.make_async_copy(out_at.at[t], new_v.at[0, t], sems.at[t]))
+        stores[t].start()
+    for store in stores:
+        store.wait()
 
 
 SMEM = pl.BlockSpec(memory_space=pltpu.SMEM)
 VMEM = pl.BlockSpec(memory_space=pltpu.VMEM)
-LIMIT = 40 * 1024 * 1024
+ANY = pl.BlockSpec(memory_space=pl.ANY)
+LIMIT = 16 * 1024 * 1024
 
 
 def left_side(tile_rank, row_rank, target_rank, place, tile_u, near, far):
@@ -164,7 +170,7 @@
         ],
         compiler_params=pltpu.CompilerParams(vmem_limit_bytes=LIMIT),
         cost_estimate=pl.CostEstimate(
-            flops=int(1e10), bytes_accessed=int(40e6), transcendentals=0
+            flops=int(17e9), bytes_accessed=int(40e6), transcendentals=int(1e12)
         ),
         name="left_side",
     )(tile_rank, row_rank, target_rank, place, tile_u, near, far)
@@ -176,7 +182,11 @@
         right_kernel,
         out_shape=jax.ShapeDtypeStruct((1, tiles, order, width), BF16),
         in_specs=[SMEM] * 2 + [VMEM] * 5,
-        out_specs=VMEM,
+        out_specs=ANY,
+        scratch_shapes=[
+            pltpu.VMEM((tiles, order, width), BF16),
+            pltpu.SemaphoreType.DMA((tiles,)),
+        ],
         compiler_params=pltpu.CompilerParams(vmem_limit_bytes=LIMIT),
         cost_estimate=pl.CostEstimate(
             flops=int(2e9), bytes_accessed=int(10e6), transcendentals=0
@@ -185,9 +195,74 @@
     )(band_rank, place, tile_v, near, far, panels, head)
 
 
-def from_all(x, axes, size):
-    copies = jnp.broadcast_to(x[None], (size,) + x.shape)
-    return lax.all_to_all(copies, axes, 0, 0, tiled=True)
+def copies_kernel(line, out):
+    for k in range(out.shape[0]):
+        out[k] = line[...]
+
+
+def copies_of(line, size):
+    return pl.pallas_call(
+        copies_kernel,
+        out_shape=jax.ShapeDtypeStruct((size,) + line.shape, line.dtype),
+        in_specs=[VMEM],
+        out_specs=VMEM,
+        compiler_params=pltpu.CompilerParams(vmem_limit_bytes=LIMIT),
+        name="copies",
+    )(line)
+
+
+def prepare_kernel(panel_u, panel_v, row_u, row_v, line, row, share, sems):
+    sources = (panel_u, panel_v, row_u.at[0], row_v.at[0])
+    targets = (share.at[0], share.at[1], row.at[0, 0], row.at[0, 1])
+    copies = [
+        pltpu.make_async_copy(sources[k], targets[k], sems.at[k]) for k in range(len(sources))
+    ]
+    for copy in copies:
+        copy.start()
+    copies[0].wait()
+    copies[1].wait()
+    both = share[...].astype(F32).reshape(line.shape[1:]).astype(BF16)
+    line[...] = jnp.broadcast_to(both[None], line.shape)
+    copies[2].wait()
+    copies[3].wait()
+
+
+def prepare(panel_u, panel_v, row_u, row_v, size):
+    tiles, share, width = panel_u.shape
+    return pl.pallas_call(
+        prepare_kernel,
+        out_shape=(
+            jax.ShapeDtypeStruct((size, 2 * tiles * share, width), BF16),
+            jax.ShapeDtypeStruct((1, 2) + row_u.shape[1:], BF16),
+        ),
+        in_specs=[ANY] * 4,
+        out_specs=(VMEM, VMEM),
+        scratch_shapes=[
+            pltpu.VMEM((2,) + panel_u.shape, BF16),
+            pltpu.SemaphoreType.DMA((4,)),
+        ],
+        compiler_params=pltpu.CompilerParams(vmem_limit_bytes=None),
+        cost_estimate=pl.CostEstimate(
+            flops=int(1e8), bytes_accessed=int(1e6), transcendentals=0
+        ),
+        name="prepare",
+    )(panel_u, panel_v, row_u, row_v)
+
+
+def join_kernel(row, across, near):
+    near[0] = row[0]
+    near[1] = across[0]
+
+
+def join(row, across):
+    return pl.pallas_call(
+        join_kernel,
+        out_shape=jax.ShapeDtypeStruct((2,) + row.shape[1:], row.dtype),
+        in_specs=[VMEM] * 2,
+        out_specs=VMEM,
+        compiler_params=pltpu.CompilerParams(vmem_limit_bytes=LIMIT),
+        name="join",
+    )(row, across)
 
 
 def swap(x, axis):
@@ -198,12 +273,13 @@
     tile_u, tile_v, tile_rank, panel_u, panel_v, band_rank, row_u, row_v, row_rank, target_rank
 ):
     tiles, share, width = panel_u.shape
-    row = jnp.concatenate([row_u, row_v], axis=0)
-    panel = jnp.concatenate([panel_u, panel_v], axis=0).reshape(2 * tiles * share, width)
+    copies, row = prepare(panel_u, panel_v, row_u, row_v, 8)
     across = swap(row, "zh")
-    line = from_all(panel, "z", 8)
-    panels = from_all(line, ("y", "x"), 16)
-    near = jnp.stack([row, across])
+    line = lax.all_to_all(copies, "z", 0, 0, tiled=True)
+    copies = copies_of(line, 16)
+    panels = lax.all_to_all(copies, ("y", "x"), 0, 0, tiled=True)
+    near = join(row, across)
+    panels = lax.all_to_all(copies, ("y", "x"), 0, 0, tiled=True)
     far = swap(near, "core")
     place = jnp.stack([lax.axis_index("zh"), lax.axis_index("core")]).astype(jnp.int32)
     new_u, head = left_side(tile_rank, row_rank, target_rank, place, tile_u[0], near, far)

time: 79.6 us -> 67.1 us (0.84)
  the two profiles are of different devices: /device:TPU:1 before, /device:TPU:32 now
where the time goes in v2:
time: 67.1 us; the launch traced here: 66.7 us
  starting transfers between devices  30 us (45%)
  Pallas kernels  18 us (27%)
  waiting for transfers between devices  17.3 us (26%)
  between operations  1.37 us (2%)
    all_to_all x1, waiting for transfers between devices, on_device(): panels = lax.all_to_all(copies, ('y', 'x'), 0, 0, tiled=True)  13.5 us
    all_to_all x1, starting transfers between devices, on_device(): line = lax.all_to_all(copies, 'z', 0, 0, tiled=True)  12.6 us
    pallas_call x1, Pallas kernels, left_side(): pl.pallas_call(left_kernel, out_shape=(jax.ShapeDtypeStruct((1, tiles, or...  10.7 us
    ppermute x2, starting transfers between devices, swap(): return lax.ppermute(x, axis, [(0, 1), (1, 0)])  10.1 us
    all_to_all x1, starting transfers between devices, on_device(): panels = lax.all_to_all(copies, ('y', 'x'), 0, 0, tiled=True)  7.23 us
    pallas_call x1, Pallas kernels, right_side(): pl.pallas_call(right_kernel, out_shape=jax.ShapeDtypeStruct((1, tiles, or...  4.1 us
    all_to_all x1, waiting for transfers between devices, on_device(): line = lax.all_to_all(copies, 'z', 0, 0, tiled=True)  3.05 us
    pallas_call x1, Pallas kernels, prepare(): pl.pallas_call(prepare_kernel, out_shape=(jax.ShapeDtypeStruct((size, 2 *...  1.64 us
  transfers between devices with their start and end apart: 4, of which 3 were waited for; matrix products, arithmetic and copies ran while one was open for 0% of the time, Pallas kernels for 18%

profile of v2, /device:TPU:32, one launch (start us, length us, event | category | flops | bytes accessed | tf_op | source)
XLA Modules:
  0.0 66.7 jit_solution(14361178242802237256)
XLA Ops:
  0.6 1.6 %prepare.1 = (bf16[8,64,128]{2,1,0:T(8,128)(2,1)}, bf16[1,2,256,128]{3,2,1,0:T(8,128)(2,1)}) custom-call(bf16[4,8,128]{2,1,0:T(8,128)(2,1)} %panel_u.1, bf16[4,8,128]{2,1,0:T(8,128)(2,1)} %panel_v.1, bf16[1,256,128]{2,1,0:T(8,128)(2,1)} %row_u.1, bf16[1,256,128]{2,1,0:T(8,128)(2,1)} %row_v.1), custom_call_target="tpu_custom_call" | custom-call | flops 100000000 | bytes 1000000 | tf_op jit(solution)/shard_map/prepare/pallas_call | solution.py:232
  2.3 12.6 %all-to-all-start = ((bf16[8,64,128]{2,1,0:T(8,128)(2,1)}), bf16[8,64,128]{2,1,0:T(8,128)(2,1)S(1)}, u32[]{:S(2)}, u32[]{:S(2)}) async-start(bf16[8,64,128]{2,1,0:T(8,128)(2,1)} %get-tuple-element.8), calls=%async_computation | async-start | bytes 262144 | tf_op jit(solution)/shard_map/all_to_all | solution.py:278
  14.9 8.2 %collective-permute-start = (bf16[1,2,256,128]{3,2,1,0:T(8,128)(2,1)}, bf16[1,2,256,128]{3,2,1,0:T(8,128)(2,1)S(1)}, u32[]{:S(2)}, u32[]{:S(2)}) collective-permute-start(bf16[1,2,256,128]{3,2,1,0:T(8,128)(2,1)} %get-tuple-element.6.row), channel_id=1, source_target_pairs={{0,2},{2,0},{1,3},{3,1},{4,6},{6,4},{5,7},{7,5},{8,10},{10,8},{9,1... | collective-permute-start | bytes 393224 | tf_op jit(solution)/shard_map/ppermute | solution.py:269
  23.1 3.1 %all-to-all-done.line = bf16[8,64,128]{2,1,0:T(8,128)(2,1)S(1)} async-done(((bf16[8,64,128]{2,1,0:T(8,128)(2,1)}), bf16[8,64,128]{2,1,0:T(8,128)(2,1)S(1)}, u32[]{:S(2)}, u32[]{:S(2)}) %all-to-all-start) | async-done | bytes 131104 | tf_op jit(solution)/shard_map/all_to_all | solution.py:278
  26.2 1.6 %copies.1 = bf16[16,8,64,128]{3,2,1,0:T(8,128)(2,1)} custom-call(bf16[8,64,128]{2,1,0:T(8,128)(2,1)S(1)} %all-to-all-done.line), custom_call_target="tpu_custom_call" | custom-call | tf_op jit(solution)/shard_map/copies/pallas_call | solution.py:204
  27.8 0.0 copy-start
  27.8 0.0 copy-start.1
  27.8 0.0 copy-start.3
  27.8 0.0 copy-start.4
  27.8 7.2 %all-to-all-start.1 = ((bf16[16,8,64,128]{3,2,1,0:T(8,128)(2,1)}), bf16[16,8,64,128]{3,2,1,0:T(8,128)(2,1)}, u32[]{:S(2)}, u32[]{:S(2)}) async-start(bf16[16,8,64,128]{3,2,1,0:T(8,128)(2,1)} %copies.1), calls=%async_computation.1 | async-start | bytes 4194304 | tf_op jit(solution)/shard_map/all_to_all | solution.py:282
  35.0 0.0 collective-permute-done.across
  35.0 0.0 copy-done
  35.1 1.9 %collective-permute-start.1 = (bf16[2,2,256,128]{3,2,1,0:T(8,128)(2,1)S(1)}, bf16[2,2,256,128]{3,2,1,0:T(8,128)(2,1)S(1)}, u32[]{:S(2)}, u32[]{:S(2)}) collective-permute-start(bf16[2,2,256,128]{3,2,1,0:T(8,128)(2,1)S(1)} %join.1.near), channel_id=1, source_target_pairs={{0,1},{1,0},{2,3},{3,2},{4,5},{5,4},{6,7},{7,6},{8,9},{9,8},{10,11... | collective-permute-start | bytes 786440 | tf_op jit(solution)/shard_map/ppermute | solution.py:269
  37.6 0.1 pad_add_fusion.place
  37.7 0.8 %collective-permute-done.1.far = bf16[2,2,256,128]{3,2,1,0:T(8,128)(2,1)S(1)} collective-permute-done((bf16[2,2,256,128]{3,2,1,0:T(8,128)(2,1)S(1)}, bf16[2,2,256,128]{3,2,1,0:T(8,128)(2,1)S(1)}, u32[]{:S(2)}, u32[]{:S(2)}) %collective-permute-start.1) | collective-permute-done | bytes 262176 | tf_op jit(solution)/shard_map/ppermute | solution.py:269
  38.5 0.0 copy-done.1
  38.5 0.0 copy-done.3
  38.5 0.0 copy-done.4
  38.5 0.0 copy-start.2
  38.5 0.0 copy-start.5
  38.5 10.7 %left_side.1 = (bf16[1,4,1024,128]{3,2,1,0:T(8,128)(2,1)}, f32[4,128,256]{2,1,0:T(8,128)S(1)}) custom-call(s32[1,4]{1,0:T(1,128)S(1)} %copy-done.3, s32[1]{0:T(128)S(6)} %copy.12.row_rank, s32[1,4]{1,0:T(1,128)S(1)} %copy-done.4, s32[2]{0:T(128)S(1)} %pad_add_fusion.place, bf16[4,1024,128]{2,1,0:T(8,128)(2,1)S(1)} %bitcast.5, ...), custom_call_target="tpu_custom_call" | custom-call | flops 16999999488 | bytes 40000000 | tf_op jit(solution)/shard_map/left_side/pallas_call | solution.py:159
  49.2 13.5 %all-to-all-done.1 = bf16[16,8,64,128]{3,2,1,0:T(8,128)(2,1)} async-done(((bf16[16,8,64,128]{3,2,1,0:T(8,128)(2,1)}), bf16[16,8,64,128]{3,2,1,0:T(8,128)(2,1)}, u32[]{:S(2)}, u32[]{:S(2)}) %all-to-all-start.1) | async-done | bytes 2097184 | tf_op jit(solution)/shard_map/all_to_all | solution.py:282
  62.6 0.0 copy-done.2
  62.6 0.0 copy-done.5
  62.6 4.1 %right_side.1 = bf16[1,4,1024,128]{3,2,1,0:T(8,128)(2,1)} custom-call(s32[4]{0:T(128)S(1)} %copy-done.5, s32[2]{0:T(128)S(1)} %pad_add_fusion.place, bf16[4,1024,128]{2,1,0:T(8,128)(2,1)S(1)} %bitcast.6, bf16[2,2,256,128]{3,2,1,0:T(8,128)(2,1)S(1)} %join.1.near, bf16[2,2,256,128]{3,2,1,0:T(8,128)(2,1)S(1)} %collective-permute-done.1.far, ...), custom_call_target="tpu_custom_call" | custom-call | flops 2000000000 | bytes 10000000 | tf_op jit(solution)/shard_map/right_side/pallas_call | solution.py:181
  (1 shorter events, 0.0 us)
Async XLA Ops:
  2.3 23.9 %all-to-all-start = ((bf16[8,64,128]{2,1,0:T(8,128)(2,1)}), bf16[8,64,128]{2,1,0:T(8,128)(2,1)S(1)}, u32[]{:S(2)}, u32[]{:S(2)}) async-start(bf16[8,64,128]{2,1,0:T(8,128)(2,1)} %get-tuple-element.8), calls=%async_computation | async-start | bytes 262144 | tf_op jit(solution)/shard_map/all_to_all | solution.py:278
  14.9 20.1 %collective-permute-start = (bf16[1,2,256,128]{3,2,1,0:T(8,128)(2,1)}, bf16[1,2,256,128]{3,2,1,0:T(8,128)(2,1)S(1)}, u32[]{:S(2)}, u32[]{:S(2)}) collective-permute-start(bf16[1,2,256,128]{3,2,1,0:T(8,128)(2,1)} %get-tuple-element.6.row), channel_id=1, source_target_pairs={{0,2},{2,0},{1,3},{3,1},{4,6},{6,4},{5,7},{7,5},{8,10},{10,8},{9,1... | collective-permute-start | bytes 393224 | tf_op jit(solution)/shard_map/ppermute | solution.py:269
  27.8 7.3 %copy-start = (bf16[1,2,256,128]{3,2,1,0:T(8,128)(2,1)S(1)}, bf16[1,2,256,128]{3,2,1,0:T(8,128)(2,1)}, u32[]{:S(2)}) copy-start(bf16[1,2,256,128]{3,2,1,0:T(8,128)(2,1)} %get-tuple-element.6.row) | copy-start | bytes 393220
  27.8 10.7 %copy-start.1 = (bf16[1,4,1024,128]{3,2,1,0:T(8,128)(2,1)S(1)}, bf16[1,4,1024,128]{3,2,1,0:T(8,128)(2,1)}, u32[]{:S(2)}) copy-start(bf16[1,4,1024,128]{3,2,1,0:T(8,128)(2,1)} %param.10) | copy-start | bytes 3145732
  27.8 10.7 %copy-start.3 = (s32[1,4]{1,0:T(1,128)S(1)}, s32[1,4]{1,0:T(1,128)}, u32[]{:S(2)}) copy-start(s32[1,4]{1,0:T(1,128)} %tile_rank.1) | copy-start | bytes 52
  27.8 10.7 %copy-start.4 = (s32[1,4]{1,0:T(1,128)S(1)}, s32[1,4]{1,0:T(1,128)}, u32[]{:S(2)}) copy-start(s32[1,4]{1,0:T(1,128)} %target_rank.1) | copy-start | bytes 52
  27.8 34.9 %all-to-all-start.1 = ((bf16[16,8,64,128]{3,2,1,0:T(8,128)(2,1)}), bf16[16,8,64,128]{3,2,1,0:T(8,128)(2,1)}, u32[]{:S(2)}, u32[]{:S(2)}) async-start(bf16[16,8,64,128]{3,2,1,0:T(8,128)(2,1)} %copies.1), calls=%async_computation.1 | async-start | bytes 4194304 | tf_op jit(solution)/shard_map/all_to_all | solution.py:282
  35.1 3.4 %collective-permute-start.1 = (bf16[2,2,256,128]{3,2,1,0:T(8,128)(2,1)S(1)}, bf16[2,2,256,128]{3,2,1,0:T(8,128)(2,1)S(1)}, u32[]{:S(2)}, u32[]{:S(2)}) collective-permute-start(bf16[2,2,256,128]{3,2,1,0:T(8,128)(2,1)S(1)} %join.1.near), channel_id=1, source_target_pairs={{0,1},{1,0},{2,3},{3,2},{4,5},{5,4},{6,7},{7,6},{8,9},{9,8},{10,11... | collective-permute-start | bytes 786440 | tf_op jit(solution)/shard_map/ppermute | solution.py:269
  38.5 24.1 %copy-start.2 = (bf16[1,4,1024,128]{3,2,1,0:T(8,128)(2,1)S(1)}, bf16[1,4,1024,128]{3,2,1,0:T(8,128)(2,1)}, u32[]{:S(2)}) copy-start(bf16[1,4,1024,128]{3,2,1,0:T(8,128)(2,1)} %param.11) | copy-start | bytes 3145732
  38.5 24.1 %copy-start.5 = (s32[4]{0:T(128)S(1)}, s32[4]{0:T(128)}, u32[]{:S(2)}) copy-start(s32[4]{0:T(128)} %band_rank.1) | copy-start | bytes 52

commit v3 on v2

--- a/solution.py
+++ b/solution.py
@@ -10,6 +10,7 @@
 F32, BF16 = jnp.float32, jnp.bfloat16
 HIGH = lax.Precision.HIGHEST
 STEP = 8
+ORDER = [3, 4, 2, 5, 1, 6, 0, 7]
 
 
 def dot(a, b, dims, precision=None):
@@ -121,25 +122,32 @@
     right_row = jnp.concatenate(rows, axis=0)
     lane = lax.broadcasted_iota(jnp.int32, (width, width), 1)
 
-    def panel(which):
-        found = []
-        for pair in range(0, tiles, 2):
-            at = (which * tiles + pair) * STEP
-            wide = panels[:, at : at + 2 * STEP, :].astype(F32)
-            found.append(wide[:, :STEP].reshape(order, width).astype(BF16))
-            found.append(wide[:, STEP:].reshape(order, width).astype(BF16))
-        return found
-
-    core = dot(right_row, jnp.concatenate(panel(1), axis=1), ((0,), (0,)))
-    panel_u = panel(0)
-    stores = []
+    def panel_pair(which, pair):
+        at = (which * tiles + pair) * STEP
+        wide = panels[:, at : at + 2 * STEP, :].astype(F32)
+        wide = wide.reshape(-1, len(ORDER), 2 * STEP, width)
+        wide = jnp.stack([wide[:, ORDER.index(z)] for z in range(len(ORDER))], axis=1)
+        return [
+            wide[:, :, :STEP].reshape(order, width).astype(BF16),
+            wide[:, :, STEP:].reshape(order, width).astype(BF16),
+        ]
+
+    panel_v = panel_pair(1, 0) + panel_pair(1, 2)
+    core = dot(right_row, jnp.concatenate(panel_v, axis=1), ((0,), (0,)))
+    weights = []
     for t in range(tiles):
         mixed = dot(head[t, :, width:], core[:, t * width : (t + 1) * width], ((1,), (0,)), HIGH)
         mixed = jnp.where(lane < band_rank[t], -mixed, 0.0)
         weight = jnp.concatenate([head[t, :, :width], mixed], axis=1)
         high = weight.astype(BF16)
         low = (weight - high.astype(F32)).astype(BF16)
-        both = jnp.concatenate([tile_v[t], panel_u[t]], axis=1)
+        weights.append((high, low))
+    stores = []
+    for t in range(tiles):
+        if t % 2 == 0:
+            panel_u = panel_pair(0, t)
+        high, low = weights[t]
+        both = jnp.concatenate([tile_v[t], panel_u[t % 2]], axis=1)
         value = dot(both, jnp.concatenate([high, low], axis=0), ((1,), (1,)))
         out_at[t] = (value[:, :width] + value[:, width:]).astype(BF16)
         stores.append(pltpu.make_async_copy(out_at.at[t], new_v.at[0, t], sems.at[t]))
@@ -195,9 +203,12 @@
     )(band_rank, place, tile_v, near, far, panels, head)
 
 
-def copies_kernel(line, out):
-    for k in range(out.shape[0]):
-        out[k] = line[...]
+def copies_kernel(line, out, sems):
+    stores = [pltpu.make_async_copy(line, out.at[k], sems.at[k]) for k in range(out.shape[0])]
+    for store in stores:
+        store.start()
+    for store in stores:
+        store.wait()
 
 
 def copies_of(line, size):
@@ -205,48 +216,48 @@
         copies_kernel,
         out_shape=jax.ShapeDtypeStruct((size,) + line.shape, line.dtype),
         in_specs=[VMEM],
-        out_specs=VMEM,
+        out_specs=ANY,
+        scratch_shapes=[pltpu.SemaphoreType.DMA((size,))],
         compiler_params=pltpu.CompilerParams(vmem_limit_bytes=LIMIT),
         name="copies",
     )(line)
 
 
-def prepare_kernel(panel_u, panel_v, row_u, row_v, line, row, share, sems):
-    sources = (panel_u, panel_v, row_u.at[0], row_v.at[0])
-    targets = (share.at[0], share.at[1], row.at[0, 0], row.at[0, 1])
-    copies = [
-        pltpu.make_async_copy(sources[k], targets[k], sems.at[k]) for k in range(len(sources))
+def prepare_kernel(panel_u, panel_v, line, share, both, sems):
+    loads = [
+        pltpu.make_async_copy(x, share.at[k], sems.at[k]) for k, x in enumerate((panel_u, panel_v))
     ]
-    for copy in copies:
-        copy.start()
-    copies[0].wait()
-    copies[1].wait()
-    both = share[...].astype(F32).reshape(line.shape[1:]).astype(BF16)
-    line[...] = jnp.broadcast_to(both[None], line.shape)
-    copies[2].wait()
-    copies[3].wait()
-
-
-def prepare(panel_u, panel_v, row_u, row_v, size):
+    for load in loads:
+        load.start()
+    for load in loads:
+        load.wait()
+    both[...] = share[...].astype(F32).reshape(both.shape).astype(BF16)
+    stores = [pltpu.make_async_copy(both, line.at[k], sems.at[k]) for k in range(line.shape[0])]
+    for store in stores:
+        store.start()
+    for store in stores:
+        store.wait()
+
+
+def prepare(panel_u, panel_v, size):
     tiles, share, width = panel_u.shape
+    rows = 2 * tiles * share
     return pl.pallas_call(
         prepare_kernel,
-        out_shape=(
-            jax.ShapeDtypeStruct((size, 2 * tiles * share, width), BF16),
-            jax.ShapeDtypeStruct((1, 2) + row_u.shape[1:], BF16),
-        ),
-        in_specs=[ANY] * 4,
-        out_specs=(VMEM, VMEM),
+        out_shape=jax.ShapeDtypeStruct((size, rows, width), BF16),
+        in_specs=[ANY] * 2,
+        out_specs=ANY,
         scratch_shapes=[
             pltpu.VMEM((2,) + panel_u.shape, BF16),
-            pltpu.SemaphoreType.DMA((4,)),
+            pltpu.VMEM((rows, width), BF16),
+            pltpu.SemaphoreType.DMA((size,)),
         ],
         compiler_params=pltpu.CompilerParams(vmem_limit_bytes=None),
         cost_estimate=pl.CostEstimate(
             flops=int(1e8), bytes_accessed=int(1e6), transcendentals=0
         ),
         name="prepare",
-    )(panel_u, panel_v, row_u, row_v)
+    )(panel_u, panel_v)
 
 
 def join_kernel(row, across, near):
@@ -273,9 +284,10 @@
     tile_u, tile_v, tile_rank, panel_u, panel_v, band_rank, row_u, row_v, row_rank, target_rank
 ):
     tiles, share, width = panel_u.shape
-    copies, row = prepare(panel_u, panel_v, row_u, row_v, 8)
+    copies = prepare(panel_u, panel_v, 8)
+    row = jnp.stack([row_u, row_v], axis=1)
     across = swap(row, "zh")
-    line = lax.all_to_all(copies, "z", 0, 0, tiled=True)
+    line = lax.all_to_all(copies, "z", 0, 0, axis_index_groups=[ORDER], tiled=True)
     copies = copies_of(line, 16)
     panels = lax.all_to_all(copies, ("y", "x"), 0, 0, tiled=True)
     near = join(row, across)

time: 67.1 us -> 65.7 us (0.979)
  the two profiles are of different devices: /device:TPU:32 before, /device:TPU:24 now
where the time goes in v3:
time: 65.7 us; the launch traced here: 65.3 us
  starting transfers between devices  30.6 us (47%)
  Pallas kernels  17.3 us (26%)
  waiting for transfers between devices  15 us (23%)
  between operations  1.38 us (2%)
  other arithmetic  0.96 us (1%)
    all_to_all x1, waiting for transfers between devices, on_device(): panels = lax.all_to_all(copies, ('y', 'x'), 0, 0, tiled=True)  14.2 us
    all_to_all x1, starting transfers between devices, on_device(): lax.all_to_all(copies, 'z', 0, 0, axis_index_groups=[ORDER], tiled=True)  13.1 us
    pallas_call x1, Pallas kernels, left_side(): pl.pallas_call(left_kernel, out_shape=(jax.ShapeDtypeStruct((1, tiles, or...  10.7 us
    ppermute x2, starting transfers between devices, swap(): return lax.ppermute(x, axis, [(0, 1), (1, 0)])  10.1 us
    all_to_all x1, starting transfers between devices, on_device(): panels = lax.all_to_all(copies, ('y', 'x'), 0, 0, tiled=True)  7.31 us
    pallas_call x1, Pallas kernels, right_side(): pl.pallas_call(right_kernel, out_shape=jax.ShapeDtypeStruct((1, tiles, or...  3.77 us
    pallas_call x1, Pallas kernels, copies_of(): pl.pallas_call(copies_kernel, out_shape=jax.ShapeDtypeStruct((size,) + li...  1.46 us
    pallas_call x1, Pallas kernels, prepare(): pl.pallas_call(prepare_kernel, out_shape=jax.ShapeDtypeStruct((size, rows...  1.43 us
  transfers between devices with their start and end apart: 4, of which 2 were waited for; matrix products, arithmetic and copies ran while one was open for 1% of the time, Pallas kernels for 19%

profile of v3, /device:TPU:24, one launch (start us, length us, event | category | flops | bytes accessed | tf_op | source)
XLA Modules:
  0.0 65.3 jit_solution(6357928204355294241)
XLA Ops:
  0.6 1.4 %prepare.1 = bf16[8,64,128]{2,1,0:T(8,128)(2,1)} custom-call(bf16[4,8,128]{2,1,0:T(8,128)(2,1)} %panel_u.1, bf16[4,8,128]{2,1,0:T(8,128)(2,1)} %panel_v.1), custom_call_target="tpu_custom_call" | custom-call | flops 100000000 | bytes 1000000 | tf_op jit(solution)/shard_map/prepare/pallas_call | solution.py:245
  2.1 13.1 %all-to-all-start = ((bf16[8,64,128]{2,1,0:T(8,128)(2,1)}), bf16[8,64,128]{2,1,0:T(8,128)(2,1)S(1)}, u32[]{:S(2)}, u32[]{:S(2)}) async-start(bf16[8,64,128]{2,1,0:T(8,128)(2,1)} %prepare.1), calls=%async_computation | async-start | bytes 262144 | tf_op jit(solution)/shard_map/all_to_all | solution.py:290
  15.2 0.9 %pad_maximum_fusion.row = bf16[1,2,256,128]{3,2,1,0:T(8,128)(2,1)S(1)} fusion(bf16[1,1,256,128]{3,2,1,0:T(8,128)(2,1)} %bitcast.9, bf16[1,1,256,128]{3,2,1,0:T(8,128)(2,1)} %bitcast.10), kind=kLoop, calls=%fused_computation | loop fusion | flops 65536 | bytes 262144 | tf_op jit(solution)/shard_map/stack | solution.py:288
  16.1 8.2 %collective-permute-start = (bf16[1,2,256,128]{3,2,1,0:T(8,128)(2,1)S(1)}, bf16[1,2,256,128]{3,2,1,0:T(8,128)(2,1)S(1)}, u32[]{:S(2)}, u32[]{:S(2)}) collective-permute-start(bf16[1,2,256,128]{3,2,1,0:T(8,128)(2,1)S(1)} %pad_maximum_fusion.row), channel_id=1, source_target_pairs={{0,2},{2,0},{1,3},{3,1},{4,6},{6,4},{5,7},{7,5},{8,10},{10,8},{9,1... | collective-permute-start | bytes 393224 | tf_op jit(solution)/shard_map/ppermute | solution.py:280
  24.3 0.0 all-to-all-done.line
  24.3 1.5 %copies.1 = bf16[16,8,64,128]{3,2,1,0:T(8,128)(2,1)} custom-call(bf16[8,64,128]{2,1,0:T(8,128)(2,1)S(1)} %all-to-all-done.line), custom_call_target="tpu_custom_call" | custom-call | tf_op jit(solution)/shard_map/copies/pallas_call | solution.py:215
  25.8 0.0 copy-start
  25.8 0.0 copy-start.2
  25.8 0.0 copy-start.3
  25.8 7.3 %all-to-all-start.1 = ((bf16[16,8,64,128]{3,2,1,0:T(8,128)(2,1)}), bf16[16,8,64,128]{3,2,1,0:T(8,128)(2,1)}, u32[]{:S(2)}, u32[]{:S(2)}) async-start(bf16[16,8,64,128]{3,2,1,0:T(8,128)(2,1)} %copies.1), calls=%async_computation.1 | async-start | bytes 4194304 | tf_op jit(solution)/shard_map/all_to_all | solution.py:294
  33.1 0.0 collective-permute-done.across
  33.1 1.9 %collective-permute-start.1 = (bf16[2,2,256,128]{3,2,1,0:T(8,128)(2,1)S(1)}, bf16[2,2,256,128]{3,2,1,0:T(8,128)(2,1)S(1)}, u32[]{:S(2)}, u32[]{:S(2)}) collective-permute-start(bf16[2,2,256,128]{3,2,1,0:T(8,128)(2,1)S(1)} %join.1.near), channel_id=1, source_target_pairs={{0,1},{1,0},{2,3},{3,2},{4,5},{5,4},{6,7},{7,6},{8,9},{9,8},{10,11... | collective-permute-start | bytes 786440 | tf_op jit(solution)/shard_map/ppermute | solution.py:280
  35.7 0.1 pad_add_fusion.place
  35.8 0.8 %collective-permute-done.1.far = bf16[2,2,256,128]{3,2,1,0:T(8,128)(2,1)S(1)} collective-permute-done((bf16[2,2,256,128]{3,2,1,0:T(8,128)(2,1)S(1)}, bf16[2,2,256,128]{3,2,1,0:T(8,128)(2,1)S(1)}, u32[]{:S(2)}, u32[]{:S(2)}) %collective-permute-start.1) | collective-permute-done | bytes 262176 | tf_op jit(solution)/shard_map/ppermute | solution.py:280
  36.6 0.0 copy-done
  36.6 0.0 copy-done.2
  36.6 0.0 copy-done.3
  36.6 0.0 copy-start.1
  36.6 0.0 copy-start.4
  36.6 10.7 %left_side.1 = (bf16[1,4,1024,128]{3,2,1,0:T(8,128)(2,1)}, f32[4,128,256]{2,1,0:T(8,128)S(1)}) custom-call(s32[1,4]{1,0:T(1,128)S(1)} %copy-done.2, s32[1]{0:T(128)S(6)} %copy.12.row_rank, s32[1,4]{1,0:T(1,128)S(1)} %copy-done.3, s32[2]{0:T(128)S(1)} %pad_add_fusion.place, bf16[4,1024,128]{2,1,0:T(8,128)(2,1)S(1)} %bitcast.7, ...), custom_call_target="tpu_custom_call" | custom-call | flops 16999999488 | bytes 40000000 | tf_op jit(solution)/shard_map/left_side/pallas_call | solution.py:167
  47.3 14.2 %all-to-all-done.1 = bf16[16,8,64,128]{3,2,1,0:T(8,128)(2,1)} async-done(((bf16[16,8,64,128]{3,2,1,0:T(8,128)(2,1)}), bf16[16,8,64,128]{3,2,1,0:T(8,128)(2,1)}, u32[]{:S(2)}, u32[]{:S(2)}) %all-to-all-start.1) | async-done | bytes 2097184 | tf_op jit(solution)/shard_map/all_to_all | solution.py:294
  61.5 0.0 copy-done.1
  61.5 0.0 copy-done.4
  61.5 3.8 %right_side.1 = bf16[1,4,1024,128]{3,2,1,0:T(8,128)(2,1)} custom-call(s32[4]{0:T(128)S(1)} %copy-done.4, s32[2]{0:T(128)S(1)} %pad_add_fusion.place, bf16[4,1024,128]{2,1,0:T(8,128)(2,1)S(1)} %bitcast.8, bf16[2,2,256,128]{3,2,1,0:T(8,128)(2,1)S(1)} %join.1.near, bf16[2,2,256,128]{3,2,1,0:T(8,128)(2,1)S(1)} %collective-permute-done.1.far, ...), custom_call_target="tpu_custom_call" | custom-call | flops 2000000000 | bytes 10000000 | tf_op jit(solution)/shard_map/right_side/pallas_call | solution.py:189
  (1 shorter events, 0.0 us)
Async XLA Ops:
  2.1 22.2 %all-to-all-start = ((bf16[8,64,128]{2,1,0:T(8,128)(2,1)}), bf16[8,64,128]{2,1,0:T(8,128)(2,1)S(1)}, u32[]{:S(2)}, u32[]{:S(2)}) async-start(bf16[8,64,128]{2,1,0:T(8,128)(2,1)} %prepare.1), calls=%async_computation | async-start | bytes 262144 | tf_op jit(solution)/shard_map/all_to_all | solution.py:290
  16.1 17.1 %collective-permute-start = (bf16[1,2,256,128]{3,2,1,0:T(8,128)(2,1)S(1)}, bf16[1,2,256,128]{3,2,1,0:T(8,128)(2,1)S(1)}, u32[]{:S(2)}, u32[]{:S(2)}) collective-permute-start(bf16[1,2,256,128]{3,2,1,0:T(8,128)(2,1)S(1)} %pad_maximum_fusion.row), channel_id=1, source_target_pairs={{0,2},{2,0},{1,3},{3,1},{4,6},{6,4},{5,7},{7,5},{8,10},{10,8},{9,1... | collective-permute-start | bytes 393224 | tf_op jit(solution)/shard_map/ppermute | solution.py:280
  25.8 10.8 %copy-start = (bf16[1,4,1024,128]{3,2,1,0:T(8,128)(2,1)S(1)}, bf16[1,4,1024,128]{3,2,1,0:T(8,128)(2,1)}, u32[]{:S(2)}) copy-start(bf16[1,4,1024,128]{3,2,1,0:T(8,128)(2,1)} %param.10) | copy-start | bytes 3145732
  25.8 10.8 %copy-start.2 = (s32[1,4]{1,0:T(1,128)S(1)}, s32[1,4]{1,0:T(1,128)}, u32[]{:S(2)}) copy-start(s32[1,4]{1,0:T(1,128)} %tile_rank.1) | copy-start | bytes 52
  25.8 10.8 %copy-start.3 = (s32[1,4]{1,0:T(1,128)S(1)}, s32[1,4]{1,0:T(1,128)}, u32[]{:S(2)}) copy-start(s32[1,4]{1,0:T(1,128)} %target_rank.1) | copy-start | bytes 52
  25.8 35.7 %all-to-all-start.1 = ((bf16[16,8,64,128]{3,2,1,0:T(8,128)(2,1)}), bf16[16,8,64,128]{3,2,1,0:T(8,128)(2,1)}, u32[]{:S(2)}, u32[]{:S(2)}) async-start(bf16[16,8,64,128]{3,2,1,0:T(8,128)(2,1)} %copies.1), calls=%async_computation.1 | async-start | bytes 4194304 | tf_op jit(solution)/shard_map/all_to_all | solution.py:294
  33.1 3.4 %collective-permute-start.1 = (bf16[2,2,256,128]{3,2,1,0:T(8,128)(2,1)S(1)}, bf16[2,2,256,128]{3,2,1,0:T(8,128)(2,1)S(1)}, u32[]{:S(2)}, u32[]{:S(2)}) collective-permute-start(bf16[2,2,256,128]{3,2,1,0:T(8,128)(2,1)S(1)} %join.1.near), channel_id=1, source_target_pairs={{0,1},{1,0},{2,3},{3,2},{4,5},{5,4},{6,7},{7,6},{8,9},{9,8},{10,11... | collective-permute-start | bytes 786440 | tf_op jit(solution)/shard_map/ppermute | solution.py:280
  36.6 24.9 %copy-start.1 = (bf16[1,4,1024,128]{3,2,1,0:T(8,128)(2,1)S(1)}, bf16[1,4,1024,128]{3,2,1,0:T(8,128)(2,1)}, u32[]{:S(2)}) copy-start(bf16[1,4,1024,128]{3,2,1,0:T(8,128)(2,1)} %param.11) | copy-start | bytes 3145732
  36.6 24.9 %copy-start.4 = (s32[4]{0:T(128)S(1)}, s32[4]{0:T(128)}, u32[]{:S(2)}) copy-start(s32[4]{0:T(128)} %band_rank.1) | copy-start | bytes 52

commit v4 on v3

--- a/solution.py
+++ b/solution.py
@@ -10,6 +10,7 @@
 F32, BF16 = jnp.float32, jnp.bfloat16
 HIGH = lax.Precision.HIGHEST
 STEP = 8
+BLOCK = 16
 ORDER = [3, 4, 2, 5, 1, 6, 0, 7]
 
 
@@ -27,23 +28,23 @@
 
 
 def spread(row):
-    return jnp.broadcast_to(row, (STEP, row.shape[1]))
+    return jnp.broadcast_to(row, (BLOCK, row.shape[1]))
 
 
 def factor_panel(panel, inverse, first):
     width = panel.shape[1]
-    sub = lax.broadcasted_iota(jnp.int32, (STEP, width), 0)
+    sub = lax.broadcasted_iota(jnp.int32, (BLOCK, width), 0)
     column = [
-        jnp.broadcast_to(panel[:, first + s : first + s + 1], (STEP, width)) for s in range(STEP)
+        jnp.broadcast_to(panel[:, first + s : first + s + 1], (BLOCK, width)) for s in range(BLOCK)
     ]
-    for s in range(STEP - 1):
+    for s in range(BLOCK - 1):
         ratio = jnp.where(sub > s, column[s] / spread(column[s][s : s + 1]), 0.0)
         panel = panel - ratio * spread(panel[s : s + 1])
         inverse = inverse - ratio * spread(inverse[s : s + 1])
-        for u in range(s + 1, STEP):
+        for u in range(s + 1, BLOCK):
             column[u] = column[u] - ratio * spread(column[u][s : s + 1])
     pivot = column[0]
-    for s in range(1, STEP):
+    for s in range(1, BLOCK):
         pivot = jnp.where(sub == s, column[s], pivot)
     scale = lax.rsqrt(pivot)
     scale = scale * (1.5 - 0.5 * pivot * scale * scale)
@@ -79,8 +80,8 @@
         tile_side = jnp.where(lane < tile_rank[0, t], side[:, :width], 0.0)
         row_side = jnp.where(lane < row_rank[0], side[:, width : 2 * width], 0.0)
         sides.append(jnp.concatenate([tile_side, row_side], axis=1))
-    for first in range(0, width, STEP):
-        later = first + STEP
+    for first in range(0, width, BLOCK):
+        later = first + BLOCK
         for t in range(tiles):
             upper, inverse = factor_panel(
                 gram[t, first:later, :width], gram[t, first:later, width:], first
@@ -223,41 +224,51 @@
     )(line)
 
 
-def prepare_kernel(panel_u, panel_v, line, share, both, sems):
-    loads = [
-        pltpu.make_async_copy(x, share.at[k], sems.at[k]) for k, x in enumerate((panel_u, panel_v))
-    ]
+def prepare_kernel(panel_u, panel_v, row_u, row_v, line, row, share, both, rows, sems):
+    sources = (panel_u, panel_v, row_u, row_v)
+    targets = (share.at[0], share.at[1], rows.at[:, 0], rows.at[:, 1])
+    loads = [pltpu.make_async_copy(sources[k], targets[k], sems.at[k]) for k in range(4)]
     for load in loads:
         load.start()
-    for load in loads:
+    for load in loads[:2]:
         load.wait()
     both[...] = share[...].astype(F32).reshape(both.shape).astype(BF16)
-    stores = [pltpu.make_async_copy(both, line.at[k], sems.at[k]) for k in range(line.shape[0])]
+    stores = [
+        pltpu.make_async_copy(both, line.at[k], sems.at[5 + k]) for k in range(line.shape[0])
+    ]
     for store in stores:
         store.start()
+    for load in loads[2:]:
+        load.wait()
+    stores.append(pltpu.make_async_copy(rows, row, sems.at[4]))
+    stores[-1].start()
     for store in stores:
         store.wait()
 
 
-def prepare(panel_u, panel_v, size):
+def prepare(panel_u, panel_v, row_u, row_v, size):
     tiles, share, width = panel_u.shape
     rows = 2 * tiles * share
     return pl.pallas_call(
         prepare_kernel,
-        out_shape=jax.ShapeDtypeStruct((size, rows, width), BF16),
-        in_specs=[ANY] * 2,
-        out_specs=ANY,
+        out_shape=(
+            jax.ShapeDtypeStruct((size, rows, width), BF16),
+            jax.ShapeDtypeStruct((1, 2) + row_u.shape[1:], BF16),
+        ),
+        in_specs=[ANY] * 4,
+        out_specs=(ANY, ANY),
         scratch_shapes=[
             pltpu.VMEM((2,) + panel_u.shape, BF16),
             pltpu.VMEM((rows, width), BF16),
-            pltpu.SemaphoreType.DMA((size,)),
+            pltpu.VMEM((1, 2) + row_u.shape[1:], BF16),
+            pltpu.SemaphoreType.DMA((5 + size,)),
         ],
         compiler_params=pltpu.CompilerParams(vmem_limit_bytes=None),
         cost_estimate=pl.CostEstimate(
             flops=int(1e8), bytes_accessed=int(1e6), transcendentals=0
         ),
         name="prepare",
-    )(panel_u, panel_v)
+    )(panel_u, panel_v, row_u, row_v)
 
 
 def join_kernel(row, across, near):
@@ -284,8 +295,7 @@
     tile_u, tile_v, tile_rank, panel_u, panel_v, band_rank, row_u, row_v, row_rank, target_rank
 ):
     tiles, share, width = panel_u.shape
-    copies = prepare(panel_u, panel_v, 8)
-    row = jnp.stack([row_u, row_v], axis=1)
+    copies, row = prepare(panel_u, panel_v, row_u, row_v, 8)
     across = swap(row, "zh")
     line = lax.all_to_all(copies, "z", 0, 0, axis_index_groups=[ORDER], tiled=True)
     copies = copies_of(line, 16)

time: 65.7 us -> 64.4 us (0.980)
  the two profiles are of different devices: /device:TPU:24 before, /device:TPU:32 now
where the time goes in v4:
time: 64.4 us; the launch traced here: 64 us
  starting transfers between devices  29.1 us (45%)
  waiting for transfers between devices  17 us (26%)
  Pallas kernels  16.4 us (25%)
  between operations  1.38 us (2%)
    all_to_all x1, waiting for transfers between devices, on_device(): panels = lax.all_to_all(copies, ('y', 'x'), 0, 0, tiled=True)  11.8 us
    all_to_all x1, starting transfers between devices, on_device(): lax.all_to_all(copies, 'z', 0, 0, axis_index_groups=[ORDER], tiled=True)  11.7 us
    ppermute x2, starting transfers between devices, swap(): return lax.ppermute(x, axis, [(0, 1), (1, 0)])  10.1 us
    pallas_call x1, Pallas kernels, left_side(): pl.pallas_call(left_kernel, out_shape=(jax.ShapeDtypeStruct((1, tiles, or...  9.48 us
    all_to_all x1, starting transfers between devices, on_device(): panels = lax.all_to_all(copies, ('y', 'x'), 0, 0, tiled=True)  7.23 us
    ppermute x2, waiting for transfers between devices, swap(): return lax.ppermute(x, axis, [(0, 1), (1, 0)])  4.04 us
    pallas_call x1, Pallas kernels, right_side(): pl.pallas_call(right_kernel, out_shape=jax.ShapeDtypeStruct((1, tiles, or...  3.78 us
    pallas_call x1, Pallas kernels, prepare(): pl.pallas_call(prepare_kernel, out_shape=(jax.ShapeDtypeStruct((size, row...  1.67 us
  transfers between devices with their start and end apart: 4, of which 4 were waited for; matrix products, arithmetic and copies ran while one was open for 0% of the time, Pallas kernels for 17%

profile of v4, /device:TPU:32, one launch (start us, length us, event | category | flops | bytes accessed | tf_op | source)
XLA Modules:
  0.0 64.0 jit_solution(7399573652294017255)
XLA Ops:
  0.6 1.7 %prepare.1 = (bf16[8,64,128]{2,1,0:T(8,128)(2,1)}, bf16[1,2,256,128]{3,2,1,0:T(8,128)(2,1)}) custom-call(bf16[4,8,128]{2,1,0:T(8,128)(2,1)} %panel_u.1, bf16[4,8,128]{2,1,0:T(8,128)(2,1)} %panel_v.1, bf16[1,256,128]{2,1,0:T(8,128)(2,1)} %row_u.1, bf16[1,256,128]{2,1,0:T(8,128)(2,1)} %row_v.1), custom_call_target="tpu_custom_call" | custom-call | flops 100000000 | bytes 1000000 | tf_op jit(solution)/shard_map/prepare/pallas_call | solution.py:252
  2.3 11.7 %all-to-all-start = ((bf16[8,64,128]{2,1,0:T(8,128)(2,1)}), bf16[8,64,128]{2,1,0:T(8,128)(2,1)S(1)}, u32[]{:S(2)}, u32[]{:S(2)}) async-start(bf16[8,64,128]{2,1,0:T(8,128)(2,1)} %get-tuple-element.8), calls=%async_computation | async-start | bytes 262144 | tf_op jit(solution)/shard_map/all_to_all | solution.py:300
  14.1 8.2 %collective-permute-start = (bf16[1,2,256,128]{3,2,1,0:T(8,128)(2,1)}, bf16[1,2,256,128]{3,2,1,0:T(8,128)(2,1)S(1)}, u32[]{:S(2)}, u32[]{:S(2)}) collective-permute-start(bf16[1,2,256,128]{3,2,1,0:T(8,128)(2,1)} %get-tuple-element.6.row), channel_id=1, source_target_pairs={{0,2},{2,0},{1,3},{3,1},{4,6},{6,4},{5,7},{7,5},{8,10},{10,8},{9,1... | collective-permute-start | bytes 393224 | tf_op jit(solution)/shard_map/ppermute | solution.py:291
  22.3 1.1 %all-to-all-done.line = bf16[8,64,128]{2,1,0:T(8,128)(2,1)S(1)} async-done(((bf16[8,64,128]{2,1,0:T(8,128)(2,1)}), bf16[8,64,128]{2,1,0:T(8,128)(2,1)S(1)}, u32[]{:S(2)}, u32[]{:S(2)}) %all-to-all-start) | async-done | bytes 131104 | tf_op jit(solution)/shard_map/all_to_all | solution.py:300
  23.4 1.4 %copies.1 = bf16[16,8,64,128]{3,2,1,0:T(8,128)(2,1)} custom-call(bf16[8,64,128]{2,1,0:T(8,128)(2,1)S(1)} %all-to-all-done.line), custom_call_target="tpu_custom_call" | custom-call | tf_op jit(solution)/shard_map/copies/pallas_call | solution.py:216
  24.9 0.0 copy-start
  24.9 0.0 copy-start.1
  24.9 0.0 copy-start.3
  24.9 0.0 copy-start.4
  24.9 7.2 %all-to-all-start.1 = ((bf16[16,8,64,128]{3,2,1,0:T(8,128)(2,1)}), bf16[16,8,64,128]{3,2,1,0:T(8,128)(2,1)}, u32[]{:S(2)}, u32[]{:S(2)}) async-start(bf16[16,8,64,128]{3,2,1,0:T(8,128)(2,1)} %copies.1), calls=%async_computation.1 | async-start | bytes 4194304 | tf_op jit(solution)/shard_map/all_to_all | solution.py:304
  32.2 3.3 %collective-permute-done.across = bf16[1,2,256,128]{3,2,1,0:T(8,128)(2,1)S(1)} collective-permute-done((bf16[1,2,256,128]{3,2,1,0:T(8,128)(2,1)}, bf16[1,2,256,128]{3,2,1,0:T(8,128)(2,1)S(1)}, u32[]{:S(2)}, u32[]{:S(2)}) %collective-permute-start) | collective-permute-done | bytes 131104 | tf_op jit(solution)/shard_map/ppermute | solution.py:291
  35.4 0.0 copy-done
  35.4 1.9 %collective-permute-start.1 = (bf16[2,2,256,128]{3,2,1,0:T(8,128)(2,1)S(1)}, bf16[2,2,256,128]{3,2,1,0:T(8,128)(2,1)S(1)}, u32[]{:S(2)}, u32[]{:S(2)}) collective-permute-start(bf16[2,2,256,128]{3,2,1,0:T(8,128)(2,1)S(1)} %join.1.near), channel_id=1, source_target_pairs={{0,1},{1,0},{2,3},{3,2},{4,5},{5,4},{6,7},{7,6},{8,9},{9,8},{10,11... | collective-permute-start | bytes 786440 | tf_op jit(solution)/shard_map/ppermute | solution.py:291
  38.0 0.1 pad_add_fusion.place
  38.1 0.8 %collective-permute-done.1.far = bf16[2,2,256,128]{3,2,1,0:T(8,128)(2,1)S(1)} collective-permute-done((bf16[2,2,256,128]{3,2,1,0:T(8,128)(2,1)S(1)}, bf16[2,2,256,128]{3,2,1,0:T(8,128)(2,1)S(1)}, u32[]{:S(2)}, u32[]{:S(2)}) %collective-permute-start.1) | collective-permute-done | bytes 262176 | tf_op jit(solution)/shard_map/ppermute | solution.py:291
  38.9 0.0 copy-done.1
  38.9 0.0 copy-done.3
  38.9 0.0 copy-done.4
  38.9 0.0 copy-start.2
  38.9 0.0 copy-start.5
  38.9 9.5 %left_side.1 = (bf16[1,4,1024,128]{3,2,1,0:T(8,128)(2,1)}, f32[4,128,256]{2,1,0:T(8,128)S(1)}) custom-call(s32[1,4]{1,0:T(1,128)S(1)} %copy-done.3, s32[1]{0:T(128)S(6)} %copy.12.row_rank, s32[1,4]{1,0:T(1,128)S(1)} %copy-done.4, s32[2]{0:T(128)S(1)} %pad_add_fusion.place, bf16[4,1024,128]{2,1,0:T(8,128)(2,1)S(1)} %bitcast.5, ...), custom_call_target="tpu_custom_call" | custom-call | flops 16999999488 | bytes 40000000 | tf_op jit(solution)/shard_map/left_side/pallas_call | solution.py:168
  48.4 11.8 %all-to-all-done.1 = bf16[16,8,64,128]{3,2,1,0:T(8,128)(2,1)} async-done(((bf16[16,8,64,128]{3,2,1,0:T(8,128)(2,1)}), bf16[16,8,64,128]{3,2,1,0:T(8,128)(2,1)}, u32[]{:S(2)}, u32[]{:S(2)}) %all-to-all-start.1) | async-done | bytes 2097184 | tf_op jit(solution)/shard_map/all_to_all | solution.py:304
  60.2 0.0 copy-done.2
  60.2 0.0 copy-done.5
  60.2 3.8 %right_side.1 = bf16[1,4,1024,128]{3,2,1,0:T(8,128)(2,1)} custom-call(s32[4]{0:T(128)S(1)} %copy-done.5, s32[2]{0:T(128)S(1)} %pad_add_fusion.place, bf16[4,1024,128]{2,1,0:T(8,128)(2,1)S(1)} %bitcast.6, bf16[2,2,256,128]{3,2,1,0:T(8,128)(2,1)S(1)} %join.1.near, bf16[2,2,256,128]{3,2,1,0:T(8,128)(2,1)S(1)} %collective-permute-done.1.far, ...), custom_call_target="tpu_custom_call" | custom-call | flops 2000000000 | bytes 10000000 | tf_op jit(solution)/shard_map/right_side/pallas_call | solution.py:190
  (1 shorter events, 0.0 us)
Async XLA Ops:
  2.3 21.1 %all-to-all-start = ((bf16[8,64,128]{2,1,0:T(8,128)(2,1)}), bf16[8,64,128]{2,1,0:T(8,128)(2,1)S(1)}, u32[]{:S(2)}, u32[]{:S(2)}) async-start(bf16[8,64,128]{2,1,0:T(8,128)(2,1)} %get-tuple-element.8), calls=%async_computation | async-start | bytes 262144 | tf_op jit(solution)/shard_map/all_to_all | solution.py:300
  14.1 21.4 %collective-permute-start = (bf16[1,2,256,128]{3,2,1,0:T(8,128)(2,1)}, bf16[1,2,256,128]{3,2,1,0:T(8,128)(2,1)S(1)}, u32[]{:S(2)}, u32[]{:S(2)}) collective-permute-start(bf16[1,2,256,128]{3,2,1,0:T(8,128)(2,1)} %get-tuple-element.6.row), channel_id=1, source_target_pairs={{0,2},{2,0},{1,3},{3,1},{4,6},{6,4},{5,7},{7,5},{8,10},{10,8},{9,1... | collective-permute-start | bytes 393224 | tf_op jit(solution)/shard_map/ppermute | solution.py:291
  24.9 10.6 %copy-start = (bf16[1,2,256,128]{3,2,1,0:T(8,128)(2,1)S(1)}, bf16[1,2,256,128]{3,2,1,0:T(8,128)(2,1)}, u32[]{:S(2)}) copy-start(bf16[1,2,256,128]{3,2,1,0:T(8,128)(2,1)} %get-tuple-element.6.row) | copy-start | bytes 393220
  24.9 14.0 %copy-start.1 = (bf16[1,4,1024,128]{3,2,1,0:T(8,128)(2,1)S(1)}, bf16[1,4,1024,128]{3,2,1,0:T(8,128)(2,1)}, u32[]{:S(2)}) copy-start(bf16[1,4,1024,128]{3,2,1,0:T(8,128)(2,1)} %param.10) | copy-start | bytes 3145732
  24.9 14.0 %copy-start.3 = (s32[1,4]{1,0:T(1,128)S(1)}, s32[1,4]{1,0:T(1,128)}, u32[]{:S(2)}) copy-start(s32[1,4]{1,0:T(1,128)} %tile_rank.1) | copy-start | bytes 52
  24.9 14.0 %copy-start.4 = (s32[1,4]{1,0:T(1,128)S(1)}, s32[1,4]{1,0:T(1,128)}, u32[]{:S(2)}) copy-start(s32[1,4]{1,0:T(1,128)} %target_rank.1) | copy-start | bytes 52
  24.9 35.3 %all-to-all-start.1 = ((bf16[16,8,64,128]{3,2,1,0:T(8,128)(2,1)}), bf16[16,8,64,128]{3,2,1,0:T(8,128)(2,1)}, u32[]{:S(2)}, u32[]{:S(2)}) async-start(bf16[16,8,64,128]{3,2,1,0:T(8,128)(2,1)} %copies.1), calls=%async_computation.1 | async-start | bytes 4194304 | tf_op jit(solution)/shard_map/all_to_all | solution.py:304
  35.4 3.4 %collective-permute-start.1 = (bf16[2,2,256,128]{3,2,1,0:T(8,128)(2,1)S(1)}, bf16[2,2,256,128]{3,2,1,0:T(8,128)(2,1)S(1)}, u32[]{:S(2)}, u32[]{:S(2)}) collective-permute-start(bf16[2,2,256,128]{3,2,1,0:T(8,128)(2,1)S(1)} %join.1.near), channel_id=1, source_target_pairs={{0,1},{1,0},{2,3},{3,2},{4,5},{5,4},{6,7},{7,6},{8,9},{9,8},{10,11... | collective-permute-start | bytes 786440 | tf_op jit(solution)/shard_map/ppermute | solution.py:291
  38.9 21.3 %copy-start.2 = (bf16[1,4,1024,128]{3,2,1,0:T(8,128)(2,1)S(1)}, bf16[1,4,1024,128]{3,2,1,0:T(8,128)(2,1)}, u32[]{:S(2)}) copy-start(bf16[1,4,1024,128]{3,2,1,0:T(8,128)(2,1)} %param.11) | copy-start | bytes 3145732
  38.9 21.3 %copy-start.5 = (s32[4]{0:T(128)S(1)}, s32[4]{0:T(128)}, u32[]{:S(2)}) copy-start(s32[4]{0:T(128)} %band_rank.1) | copy-start | bytes 52

commit v5 on v4

--- a/solution.py
+++ b/solution.py
@@ -12,6 +12,7 @@
 STEP = 8
 BLOCK = 16
 ORDER = [3, 4, 2, 5, 1, 6, 0, 7]
+PLANE = [0, 1, 3, 2, 4, 5, 7, 6, 12, 13, 15, 14, 8, 9, 11, 10]
 
 
 def dot(a, b, dims, precision=None):
@@ -126,11 +127,15 @@
     def panel_pair(which, pair):
         at = (which * tiles + pair) * STEP
         wide = panels[:, at : at + 2 * STEP, :].astype(F32)
-        wide = wide.reshape(-1, len(ORDER), 2 * STEP, width)
-        wide = jnp.stack([wide[:, ORDER.index(z)] for z in range(len(ORDER))], axis=1)
+        places = [
+            PLANE.index(p) * len(ORDER) + ORDER.index(z)
+            for p in range(len(PLANE))
+            for z in range(len(ORDER))
+        ]
+        wide = jnp.stack([wide[k] for k in places])
         return [
-            wide[:, :, :STEP].reshape(order, width).astype(BF16),
-            wide[:, :, STEP:].reshape(order, width).astype(BF16),
+            wide[:, :STEP].reshape(order, width).astype(BF16),
+            wide[:, STEP:].reshape(order, width).astype(BF16),
         ]
 
     panel_v = panel_pair(1, 0) + panel_pair(1, 2)
@@ -299,9 +304,13 @@
     across = swap(row, "zh")
     line = lax.all_to_all(copies, "z", 0, 0, axis_index_groups=[ORDER], tiled=True)
     copies = copies_of(line, 16)
-    panels = lax.all_to_all(copies, ("y", "x"), 0, 0, tiled=True)
+    panels = lax.all_to_all(
+        copies, ("y", "x"), 0, 0, axis_index_groups=[PLANE], tiled=True
+    )
     near = join(row, across)
-    panels = lax.all_to_all(copies, ("y", "x"), 0, 0, tiled=True)
+    panels = lax.all_to_all(
+        copies, ("y", "x"), 0, 0, axis_index_groups=[PLANE], tiled=True
+    )
     far = swap(near, "core")
     place = jnp.stack([lax.axis_index("zh"), lax.axis_index("core")]).astype(jnp.int32)
     new_u, head = left_side(tile_rank, row_rank, target_rank, place, tile_u[0], near, far)

time: 64.4 us -> 64 us (level)
  the two profiles are of different devices: /device:TPU:32 before, /device:TPU:12 now
where the time goes in v5:
time: 64 us; the launch traced here: 63.6 us
  starting transfers between devices  30.7 us (48%)
  Pallas kernels  16.4 us (26%)
  waiting for transfers between devices  15 us (23%)
  between operations  1.39 us (2%)
    all_to_all x1, waiting for transfers between devices, on_device(): lax.all_to_all(copies, ('y', 'x'), 0, 0, axis_index_groups=[PLANE], tiled...  13.5 us
    all_to_all x1, starting transfers between devices, on_device(): lax.all_to_all(copies, 'z', 0, 0, axis_index_groups=[ORDER], tiled=True)  13.1 us
    ppermute x2, starting transfers between devices, swap(): return lax.ppermute(x, axis, [(0, 1), (1, 0)])  10.1 us
    pallas_call x1, Pallas kernels, left_side(): pl.pallas_call(left_kernel, out_shape=(jax.ShapeDtypeStruct((1, tiles, or...  9.48 us
    all_to_all x1, starting transfers between devices, on_device(): lax.all_to_all(copies, ('y', 'x'), 0, 0, axis_index_groups=[PLANE], tiled...  7.48 us
    pallas_call x1, Pallas kernels, right_side(): pl.pallas_call(right_kernel, out_shape=jax.ShapeDtypeStruct((1, tiles, or...  3.78 us
    pallas_call x1, Pallas kernels, prepare(): pl.pallas_call(prepare_kernel, out_shape=(jax.ShapeDtypeStruct((size, row...  1.67 us
    pallas_call x1, Pallas kernels, copies_of(): pl.pallas_call(copies_kernel, out_shape=jax.ShapeDtypeStruct((size,) + li...  1.45 us
  transfers between devices with their start and end apart: 4, of which 3 were waited for; matrix products, arithmetic and copies ran while one was open for 0% of the time, Pallas kernels for 17%

profile of v5, /device:TPU:12, one launch (start us, length us, event | category | flops | bytes accessed | tf_op | source)
XLA Modules:
  0.0 63.6 jit_solution(460379170902959334)
XLA Ops:
  0.6 1.7 %prepare.1 = (bf16[8,64,128]{2,1,0:T(8,128)(2,1)}, bf16[1,2,256,128]{3,2,1,0:T(8,128)(2,1)}) custom-call(bf16[4,8,128]{2,1,0:T(8,128)(2,1)} %panel_u.1, bf16[4,8,128]{2,1,0:T(8,128)(2,1)} %panel_v.1, bf16[1,256,128]{2,1,0:T(8,128)(2,1)} %row_u.1, bf16[1,256,128]{2,1,0:T(8,128)(2,1)} %row_v.1), custom_call_target="tpu_custom_call" | custom-call | flops 100000000 | bytes 1000000 | tf_op jit(solution)/shard_map/prepare/pallas_call | solution.py:257
  2.3 13.1 %all-to-all-start = ((bf16[8,64,128]{2,1,0:T(8,128)(2,1)}), bf16[8,64,128]{2,1,0:T(8,128)(2,1)S(1)}, u32[]{:S(2)}, u32[]{:S(2)}) async-start(bf16[8,64,128]{2,1,0:T(8,128)(2,1)} %get-tuple-element.8), calls=%async_computation | async-start | bytes 262144 | tf_op jit(solution)/shard_map/all_to_all | solution.py:305
  15.4 8.2 %collective-permute-start = (bf16[1,2,256,128]{3,2,1,0:T(8,128)(2,1)}, bf16[1,2,256,128]{3,2,1,0:T(8,128)(2,1)S(1)}, u32[]{:S(2)}, u32[]{:S(2)}) collective-permute-start(bf16[1,2,256,128]{3,2,1,0:T(8,128)(2,1)} %get-tuple-element.6.row), channel_id=1, source_target_pairs={{0,2},{2,0},{1,3},{3,1},{4,6},{6,4},{5,7},{7,5},{8,10},{10,8},{9,1... | collective-permute-start | bytes 393224 | tf_op jit(solution)/shard_map/ppermute | solution.py:296
  23.6 0.7 %all-to-all-done.line = bf16[8,64,128]{2,1,0:T(8,128)(2,1)S(1)} async-done(((bf16[8,64,128]{2,1,0:T(8,128)(2,1)}), bf16[8,64,128]{2,1,0:T(8,128)(2,1)S(1)}, u32[]{:S(2)}, u32[]{:S(2)}) %all-to-all-start) | async-done | bytes 131104 | tf_op jit(solution)/shard_map/all_to_all | solution.py:305
  24.3 1.4 %copies.1 = bf16[16,8,64,128]{3,2,1,0:T(8,128)(2,1)} custom-call(bf16[8,64,128]{2,1,0:T(8,128)(2,1)S(1)} %all-to-all-done.line), custom_call_target="tpu_custom_call" | custom-call | tf_op jit(solution)/shard_map/copies/pallas_call | solution.py:221
  25.8 0.0 copy-start
  25.8 0.0 copy-start.1
  25.8 0.0 copy-start.3
  25.8 0.0 copy-start.4
  25.8 7.5 %all-to-all-start.1 = ((bf16[16,8,64,128]{3,2,1,0:T(8,128)(2,1)}), bf16[16,8,64,128]{3,2,1,0:T(8,128)(2,1)}, u32[]{:S(2)}, u32[]{:S(2)}) async-start(bf16[16,8,64,128]{3,2,1,0:T(8,128)(2,1)} %copies.1), calls=%async_computation.1 | async-start | bytes 4194304 | tf_op jit(solution)/shard_map/all_to_all | solution.py:311
  33.3 0.0 collective-permute-done.across
  33.3 0.0 copy-done
  33.4 1.9 %collective-permute-start.1 = (bf16[2,2,256,128]{3,2,1,0:T(8,128)(2,1)S(1)}, bf16[2,2,256,128]{3,2,1,0:T(8,128)(2,1)S(1)}, u32[]{:S(2)}, u32[]{:S(2)}) collective-permute-start(bf16[2,2,256,128]{3,2,1,0:T(8,128)(2,1)S(1)} %join.1.near), channel_id=1, source_target_pairs={{0,1},{1,0},{2,3},{3,2},{4,5},{5,4},{6,7},{7,6},{8,9},{9,8},{10,11... | collective-permute-start | bytes 786440 | tf_op jit(solution)/shard_map/ppermute | solution.py:296
  36.0 0.1 pad_add_fusion.place
  36.0 0.8 %collective-permute-done.1.far = bf16[2,2,256,128]{3,2,1,0:T(8,128)(2,1)S(1)} collective-permute-done((bf16[2,2,256,128]{3,2,1,0:T(8,128)(2,1)S(1)}, bf16[2,2,256,128]{3,2,1,0:T(8,128)(2,1)S(1)}, u32[]{:S(2)}, u32[]{:S(2)}) %collective-permute-start.1) | collective-permute-done | bytes 262176 | tf_op jit(solution)/shard_map/ppermute | solution.py:296
  36.8 0.0 copy-done.1
  36.8 0.0 copy-done.3
  36.8 0.0 copy-done.4
  36.8 0.0 copy-start.2
  36.8 0.0 copy-start.5
  36.8 9.5 %left_side.1 = (bf16[1,4,1024,128]{3,2,1,0:T(8,128)(2,1)}, f32[4,128,256]{2,1,0:T(8,128)S(1)}) custom-call(s32[1,4]{1,0:T(1,128)S(1)} %copy-done.3, s32[1]{0:T(128)S(6)} %copy.12.row_rank, s32[1,4]{1,0:T(1,128)S(1)} %copy-done.4, s32[2]{0:T(128)S(1)} %pad_add_fusion.place, bf16[4,1024,128]{2,1,0:T(8,128)(2,1)S(1)} %bitcast.5, ...), custom_call_target="tpu_custom_call" | custom-call | flops 16999999488 | bytes 40000000 | tf_op jit(solution)/shard_map/left_side/pallas_call | solution.py:173
  46.3 13.5 %all-to-all-done.1 = bf16[16,8,64,128]{3,2,1,0:T(8,128)(2,1)} async-done(((bf16[16,8,64,128]{3,2,1,0:T(8,128)(2,1)}), bf16[16,8,64,128]{3,2,1,0:T(8,128)(2,1)}, u32[]{:S(2)}, u32[]{:S(2)}) %all-to-all-start.1) | async-done | bytes 2097184 | tf_op jit(solution)/shard_map/all_to_all | solution.py:311
  59.8 0.0 copy-done.2
  59.8 0.0 copy-done.5
  59.8 3.8 %right_side.1 = bf16[1,4,1024,128]{3,2,1,0:T(8,128)(2,1)} custom-call(s32[4]{0:T(128)S(1)} %copy-done.5, s32[2]{0:T(128)S(1)} %pad_add_fusion.place, bf16[4,1024,128]{2,1,0:T(8,128)(2,1)S(1)} %bitcast.6, bf16[2,2,256,128]{3,2,1,0:T(8,128)(2,1)S(1)} %join.1.near, bf16[2,2,256,128]{3,2,1,0:T(8,128)(2,1)S(1)} %collective-permute-done.1.far, ...), custom_call_target="tpu_custom_call" | custom-call | flops 2000000000 | bytes 10000000 | tf_op jit(solution)/shard_map/right_side/pallas_call | solution.py:195
  (1 shorter events, 0.0 us)
Async XLA Ops:
  2.3 22.0 %all-to-all-start = ((bf16[8,64,128]{2,1,0:T(8,128)(2,1)}), bf16[8,64,128]{2,1,0:T(8,128)(2,1)S(1)}, u32[]{:S(2)}, u32[]{:S(2)}) async-start(bf16[8,64,128]{2,1,0:T(8,128)(2,1)} %get-tuple-element.8), calls=%async_computation | async-start | bytes 262144 | tf_op jit(solution)/shard_map/all_to_all | solution.py:305
  15.4 17.9 %collective-permute-start = (bf16[1,2,256,128]{3,2,1,0:T(8,128)(2,1)}, bf16[1,2,256,128]{3,2,1,0:T(8,128)(2,1)S(1)}, u32[]{:S(2)}, u32[]{:S(2)}) collective-permute-start(bf16[1,2,256,128]{3,2,1,0:T(8,128)(2,1)} %get-tuple-element.6.row), channel_id=1, source_target_pairs={{0,2},{2,0},{1,3},{3,1},{4,6},{6,4},{5,7},{7,5},{8,10},{10,8},{9,1... | collective-permute-start | bytes 393224 | tf_op jit(solution)/shard_map/ppermute | solution.py:296
  25.8 7.5 %copy-start = (bf16[1,2,256,128]{3,2,1,0:T(8,128)(2,1)S(1)}, bf16[1,2,256,128]{3,2,1,0:T(8,128)(2,1)}, u32[]{:S(2)}) copy-start(bf16[1,2,256,128]{3,2,1,0:T(8,128)(2,1)} %get-tuple-element.6.row) | copy-start | bytes 393220
  25.8 11.0 %copy-start.1 = (bf16[1,4,1024,128]{3,2,1,0:T(8,128)(2,1)S(1)}, bf16[1,4,1024,128]{3,2,1,0:T(8,128)(2,1)}, u32[]{:S(2)}) copy-start(bf16[1,4,1024,128]{3,2,1,0:T(8,128)(2,1)} %param.10) | copy-start | bytes 3145732
  25.8 11.0 %copy-start.3 = (s32[1,4]{1,0:T(1,128)S(1)}, s32[1,4]{1,0:T(1,128)}, u32[]{:S(2)}) copy-start(s32[1,4]{1,0:T(1,128)} %tile_rank.1) | copy-start | bytes 52
  25.8 11.0 %copy-start.4 = (s32[1,4]{1,0:T(1,128)S(1)}, s32[1,4]{1,0:T(1,128)}, u32[]{:S(2)}) copy-start(s32[1,4]{1,0:T(1,128)} %target_rank.1) | copy-start | bytes 52
  25.8 34.0 %all-to-all-start.1 = ((bf16[16,8,64,128]{3,2,1,0:T(8,128)(2,1)}), bf16[16,8,64,128]{3,2,1,0:T(8,128)(2,1)}, u32[]{:S(2)}, u32[]{:S(2)}) async-start(bf16[16,8,64,128]{3,2,1,0:T(8,128)(2,1)} %copies.1), calls=%async_computation.1 | async-start | bytes 4194304 | tf_op jit(solution)/shard_map/all_to_all | solution.py:311
  33.4 3.4 %collective-permute-start.1 = (bf16[2,2,256,128]{3,2,1,0:T(8,128)(2,1)S(1)}, bf16[2,2,256,128]{3,2,1,0:T(8,128)(2,1)S(1)}, u32[]{:S(2)}, u32[]{:S(2)}) collective-permute-start(bf16[2,2,256,128]{3,2,1,0:T(8,128)(2,1)S(1)} %join.1.near), channel_id=1, source_target_pairs={{0,1},{1,0},{2,3},{3,2},{4,5},{5,4},{6,7},{7,6},{8,9},{9,8},{10,11... | collective-permute-start | bytes 786440 | tf_op jit(solution)/shard_map/ppermute | solution.py:296
  36.8 23.0 %copy-start.2 = (bf16[1,4,1024,128]{3,2,1,0:T(8,128)(2,1)S(1)}, bf16[1,4,1024,128]{3,2,1,0:T(8,128)(2,1)}, u32[]{:S(2)}) copy-start(bf16[1,4,1024,128]{3,2,1,0:T(8,128)(2,1)} %param.11) | copy-start | bytes 3145732
  36.8 23.0 %copy-start.5 = (s32[4]{0:T(128)S(1)}, s32[4]{0:T(128)}, u32[]{:S(2)}) copy-start(s32[4]{0:T(128)} %band_rank.1) | copy-start | bytes 52
